TPU v7x, 256 devices: a whole 4x4x8 slice. The times are simulated.
256 devices in a mesh: space: 32 (over z, x), state: 8 (over y, core).
Axes of the slice: x: 4, y: 4, z: 8, core: 2. Of those that a mesh axis runs over, the one named last changes fastest.
Arguments:
- states: float32 [64, 524288], P('state', 'space')
- bounds: float32 [3], replicated, as said below
- element_matrix: float32 [250, 125], replicated
- elem_nodes: int32 [125, 8192], P(None, 'space'), may hold values from 0 to 20479, as said below
- face_nodes: int32 [131072], P('space'), may hold values from 0 to 16383, as said below
- kinetic: float32 [8192], P('space'), may hold values from 0.5 to 4
- potential: float32 [8192], P('space'), may hold values from -1 to 0.5
- elem_count: int32 [32], P('space'), may hold values from 64 to 256, as said below
Outputs:
- filtered: float32 [64, 524288], P('state', 'space')
- margin: float32 [64, 64], P('state')
Inputs may be any that keep to these rules, and one draw needn't show every extreme that they name: `elem_nodes`: within each partition's 256 columns, rows 0 to 99 of a column are local node indices below 16384, and rows 100 to 124 are 16384 plus a face position below 4096. The entries of one column are distinct. `face_nodes`: within each partition's 4096 entries, distinct local node indices. `elem_count`: some partition has all 256 slots live in every draw. `bounds`: a0 < lo < hi.
All inputs are finite; a program needn't handle non-finite values.
Results may differ from a plain program's by a relative error of at most 0.0018.
Values may be sent and summed in bfloat16 or wider, within the bound.
A program may use at most 128 MiB of HBM per device.

v0:
```python
import jax
import jax.numpy as jnp
from jax import lax
from jax.sharding import PartitionSpec as P

DEG = 4


def shifted(value, axis, steps):
    count = lax.axis_size(axis)
    initial, last = (max(0, -steps), min(count, count - steps))
    return lax.ppermute(value, axis, [(source, source + steps) for source in range(initial, last)])


def hamiltonian(current, elem_nodes, face_nodes, kin_live, pot_live, element_matrix):
    width = current.shape[0]
    owned_count = current.shape[1]
    face_count = face_nodes.shape[0]
    corner_count = element_matrix.shape[1]
    face_vals = current[:, face_nodes]
    ghosts = shifted(face_vals.astype(jnp.bfloat16), "space", -1).astype(face_vals.dtype)
    extended = jnp.concatenate([current, ghosts], axis=1)
    gathered = extended[:, elem_nodes]
    product = jnp.einsum("kb,sbe->ske", element_matrix, gathered, precision=lax.Precision.HIGHEST)
    contrib = kin_live * product[:, :corner_count] + pot_live * product[:, corner_count:]
    summed = (
        jnp.zeros((width, owned_count + face_count), jnp.float32).at[:, elem_nodes].add(contrib)
    )
    returned = shifted(summed[:, owned_count:].astype(jnp.bfloat16), "space", 1).astype(jnp.float32)
    return summed[:, :owned_count].at[:, face_nodes].add(returned)


def body(states, bounds, element_matrix, elem_nodes, face_nodes, kinetic, potential, elem_count):
    slot_ids = jnp.arange(kinetic.shape[0], dtype=jnp.int32)
    alive = (slot_ids < elem_count[0]).astype(jnp.float32)
    kin_live = 0.5 * kinetic * alive
    pot_live = potential * alive

    def apply_operator(block):
        return hamiltonian(block, elem_nodes, face_nodes, kin_live, pot_live, element_matrix)

    lowest, lower, upper = (bounds[0], bounds[1], bounds[2])
    half_width = (upper - lower) / 2.0
    center = (upper + lower) / 2.0
    sigma_now = half_width / (lowest - center)
    gamma_ratio = 2.0 / sigma_now
    previous = states
    current = (apply_operator(states) - center * states) * (sigma_now / half_width)
    for repeat in range(DEG - 1):
        sigma_next = 1.0 / (gamma_ratio - sigma_now)
        following = (apply_operator(current) - center * current) * (
            2.0 * sigma_next / half_width
        ) - sigma_now * sigma_next * previous
        previous = current
        current = following
        sigma_now = sigma_next
    rounded = current.astype(jnp.bfloat16)
    node_total = current.shape[1] * lax.axis_size("space")
    partial_rows = lax.dot_general(
        rounded,
        lax.all_gather(rounded, "state", axis=0, tiled=True),
        (((1,), (1,)), ((), ())),
        preferred_element_type=jnp.float32,
    )
    margin = lax.psum(partial_rows, "space") / node_total
    return (current, margin)


def solution(mesh):
    in_specs = (
        P("state", "space"),
        P(),
        P(),
        P(None, "space"),
        P("space"),
        P("space"),
        P("space"),
        P("space"),
    )
    out_specs = (P("state", "space"), P("state", None))
    return jax.shard_map(body, mesh=mesh, in_specs=in_specs, out_specs=out_specs, check_vma=False)
```

profile of v0, /device:TPU:1, one launch (start us, length us, event | category | flops | bytes accessed | tf_op | source)
XLA Modules:
  0.0 1482.0 jit_solution(14101269677599258316)
XLA Ops:
  12.0 13.8 gather_fusion
  38.1 63.1 %gather_fusion.1 = f32[32000,8]{1,0:T(8,128)} fusion(f32[8,20480]{0,1:T(8,128)} %copy.115, s32[32768]{0:T(1024)S(1)} %pad_clamp_fusion), kind=kCustom, calls=%fused_computation.1 | custom fusion | bytes 2176000 | tf_op jit(solution)/shard_map/gather | solution.py:23
  101.2 9.6 copy.116
  122.4 176.8 %scatter_custom_fusion = f32[8,20480]{0,1:T(8,128)} fusion(s32[32000]{0:T(1024)S(1)} %reshape.126, f32[32000,8]{1,0:T(8,128)} %copy.118, f32[]{:T(128)} %constant.7.clone.1), kind=kCustom, calls=%fused_computation.22 | custom fusion | flops 256000 | bytes 655872 | tf_op jit(solution)/shard_map/scatter-add | solution.py:27
  316.6 27.0 %scatter_fusion = f32[8,16384]{0,1:T(8,128)} fusion(f32[8,16384]{0,1:T(8,128)} %slice.98, s32[4096]{0:T(1024)S(1)} %get-tuple-element.12, f32[4096,8]{1,0:T(8,128)} %copy.120), kind=kCustom, calls=%fused_computation.9 | custom fusion | flops 32768 | bytes 409600 | tf_op jit(solution)/shard_map/scatter-add | solution.py:30
  352.8 13.8 gather_fusion.2
  377.3 63.1 %gather_fusion.3 = f32[32000,8]{1,0:T(8,128)} fusion(f32[8,20480]{0,1:T(8,128)} %copy.124, s32[32768]{0:T(1024)S(1)} %pad_clamp_fusion), kind=kCustom, calls=%fused_computation.3 | custom fusion | bytes 2176000 | tf_op jit(solution)/shard_map/gather | solution.py:23
  440.4 9.6 copy.125
  453.7 9.0 copy.127
  462.7 176.8 %scatter_custom_fusion.2 = f32[8,20480]{0,1:T(8,128)} fusion(s32[32000]{0:T(1024)S(1)} %reshape.126, f32[32000,8]{1,0:T(8,128)} %copy.127, f32[]{:T(128)} %constant.7.clone.1), kind=kCustom, calls=%fused_computation.20 | custom fusion | flops 256000 | bytes 655872 | tf_op jit(solution)/shard_map/scatter-add | solution.py:27
  654.1 37.7 %scatter_fusion.1 = f32[8,16384]{0,1:T(8,128)} fusion(f32[8,16384]{0,1:T(8,128)} %slice.102, s32[4096]{0:T(1024)S(1)} %get-tuple-element.12, f32[4096,8]{1,0:T(8,128)} %copy.129), kind=kCustom, calls=%fused_computation.11 | custom fusion | flops 32768 | bytes 409600 | tf_op jit(solution)/shard_map/scatter-add | solution.py:30
  701.1 13.8 gather_fusion.4
  725.7 63.1 %gather_fusion.5 = f32[32000,8]{1,0:T(8,128)} fusion(f32[8,20480]{0,1:T(8,128)} %copy.133, s32[32768]{0:T(1024)S(1)} %pad_clamp_fusion), kind=kCustom, calls=%fused_computation.5 | custom fusion | bytes 2176000 | tf_op jit(solution)/shard_map/gather | solution.py:23
  788.7 9.6 copy.134
  809.9 176.8 %scatter_custom_fusion.4 = f32[8,20480]{0,1:T(8,128)} fusion(s32[32000]{0:T(1024)S(1)} %reshape.126, f32[32000,8]{1,0:T(8,128)} %copy.136, f32[]{:T(128)} %constant.7.clone.1), kind=kCustom, calls=%fused_computation.18 | custom fusion | flops 256000 | bytes 655872 | tf_op jit(solution)/shard_map/scatter-add | solution.py:27
  1001.2 27.0 %scatter_fusion.2 = f32[8,16384]{0,1:T(8,128)} fusion(f32[8,16384]{0,1:T(8,128)} %slice.106, s32[4096]{0:T(1024)S(1)} %get-tuple-element.12, f32[4096,8]{1,0:T(8,128)} %copy.138), kind=kCustom, calls=%fused_computation.13 | custom fusion | flops 32768 | bytes 409600 | tf_op jit(solution)/shard_map/scatter-add | solution.py:30
  1037.4 13.8 gather_fusion.6
  1062.0 63.1 %gather_fusion.7 = f32[32000,8]{1,0:T(8,128)} fusion(f32[8,20480]{0,1:T(8,128)} %copy.142, s32[32768]{0:T(1024)S(1)} %pad_clamp_fusion), kind=kCustom, calls=%fused_computation.7 | custom fusion | bytes 2176000 | tf_op jit(solution)/shard_map/gather | solution.py:23
  1125.1 9.6 copy.143
  1138.3 9.0 copy.145
  1147.4 176.8 %scatter_custom_fusion.6 = f32[8,20480]{0,1:T(8,128)} fusion(s32[32000]{0:T(1024)S(1)} %reshape.126, f32[32000,8]{1,0:T(8,128)} %copy.145, f32[]{:T(128)} %constant.7.clone.1), kind=kCustom, calls=%fused_computation.16 | custom fusion | flops 256000 | bytes 655872 | tf_op jit(solution)/shard_map/scatter-add | solution.py:27
  1338.0 27.0 %scatter_fusion.3 = f32[8,16384]{0,1:T(8,128)} fusion(f32[8,16384]{0,1:T(8,128)} %slice.110, s32[4096]{0:T(1024)S(1)} %get-tuple-element.12, f32[4096,8]{1,0:T(8,128)} %copy.147), kind=kCustom, calls=%fused_computation.15 | custom fusion | flops 32768 | bytes 409600 | tf_op jit(solution)/shard_map/scatter-add | solution.py:30
  1371.6 39.0 %all-gather.2.cloned.1.call-done = bf16[64,16384]{1,0:T(8,128)(2,1)} async-done(((bf16[8,16384]{1,0:T(8,128)(2,1)}), bf16[64,16384]{1,0:T(8,128)(2,1)}) %all-gather.2.cloned.1.call-update) | async-done | bytes 2097168 | tf_op jit(solution)/shard_map/all_gather | solution.py:61
  1412.9 61.2 %psum.7 = f32[8,64]{1,0:T(8,128)S(1)} all-reduce(f32[8,64]{1,0:T(8,128)S(1)} %fusion.27), channel_id=1, replica_groups=mesh['space'=32,'state'=8] {'space'}, use_global_device_ids=true, to_apply=%region_8.0 | all-reduce | flops 512 | bytes 4096 | tf_op jit(solution)/shard_map/psum | solution.py:65
  (94 shorter events, 172.8 us)
Async XLA Ops:
  7.2 103.7 %copy-start = (f32[250,125]{1,0:T(8,128)S(1)}, f32[250,125]{1,0:T(8,128)}, u32[]{:S(2)}) copy-start(f32[250,125]{1,0:T(8,128)} %param.10) | copy-start | bytes 375004
  7.2 1403.4 %all-gather.2.cloned.1.call-start = ((), (), s32[]{:S(2)}) async-start(), calls=%async_computation | async-start | bytes 2359296 | tf_op jit(solution)/shard_map/all_gather | solution.py:61
  26.1 5.6 collective-permute-start
  122.4 182.4 %copy-start.2 = (f32[3]{0:T(128)S(1)}, f32[3]{0:T(128)}, u32[]{:S(2)}) copy-start(f32[3]{0:T(128)} %param.9) | copy-start | bytes 40
  301.2 13.4 collective-permute-start.1
  314.6 34.6 %copy-start.1 = (f32[8,16384]{1,0:T(8,128)S(1)}, f32[8,16384]{1,0:T(8,128)}, u32[]{:S(2)}) copy-start(f32[8,16384]{1,0:T(8,128)} %param.8) | copy-start | bytes 1572868
  366.9 5.0 collective-permute-start.2
  641.5 10.6 collective-permute-start.3
  715.2 5.0 collective-permute-start.4
  988.7 10.5 collective-permute-start.5
  1051.5 5.0 collective-permute-start.6
  1326.2 9.8 collective-permute-start.7
Sparse Core Ops, SparseCore 0:
  1371.7 38.8 all-gather.1
where the time goes:
time: 1500 us; the launch traced here: 1480 us
  other arithmetic  833 us (56%)
  local copies, waits for them, and re-layouts  484 us (32%)
  blocking collectives  61.2 us (4%)
  waiting for transfers between devices  51.9 us (3%)
  starting transfers between devices  22.5 us (2%)
  between operations  19.2 us (1%)
    scatter-add x4, other arithmetic, hamiltonian(): jnp.zeros((width, owned_count + face_count), jnp.float32).at[:, elem_nodes]  707 us
    gather x8, local copies, waits for them, and re-layouts, hamiltonian(): gathered = extended[:, elem_nodes]  291 us
    scatter-add x4, other arithmetic, hamiltonian(): return summed[:, :owned_count].at[:, face_nodes].add(returned)  119 us
    psum x1, blocking collectives, body(): margin = lax.psum(partial_rows, 'space') / node_total  61.2 us
    gather x4, local copies, waits for them, and re-layouts, hamiltonian(): face_vals = current[:, face_nodes]  55 us
    add x8, local copies, waits for them, and re-layouts, hamiltonian(): kin_live * product[:, :corner_count] + pot_live * product[:, corner_count:]  39.3 us
    all_gather x1, waiting for transfers between devices, body(): lax.all_gather(rounded, 'state', axis=0, tiled=True)  39 us
  transfers between devices with their start and end apart: 9, of which 5 were waited for; matrix products, arithmetic and copies ran while one was open for 2% of the time, Pallas kernels for 0%

commit v1 on v0

v1 whole, which is shorter than its diff:
```python
import functools

import jax
import jax.numpy as jnp
import numpy as np
from jax import lax
from jax.experimental import pallas as pl
from jax.experimental.pallas import tpu as pltpu
from jax.sharding import PartitionSpec as P

DEG = 4
G = 8
W = 16
LANES = G * W
KU = 5
MESH = pl.DeviceIdType.MESH
F32 = jnp.float32
BF16 = jnp.bfloat16
VMEM_LIMIT = 58 * 2**20


def expand_matrix():
    l = np.arange(LANES)[:, None]
    m = np.arange(G * LANES)[None, :]
    one = (l // W == m // LANES) & (l % W == m % W)
    return jnp.asarray(np.concatenate([one, one], 0), BF16)


def fold_matrix():
    j = np.arange(G)[:, None, None, None]
    l = np.arange(LANES)[None, None, :, None]
    m = np.arange(LANES)[None, None, None, :]
    one = (m // W == j) & (m % W == l % W)
    one = np.broadcast_to(one, (G, 2, LANES, LANES))
    return jnp.asarray(one.reshape(G * 2 * LANES, LANES), BF16)


def split(value):
    high = value.astype(BF16)
    low = (value - high.astype(F32)).astype(BF16)
    return high, low


def lane_group():
    return lax.broadcasted_iota(jnp.int32, (1, LANES), 1) // W


def merge_groups(rows):
    step = 1
    group = lane_group()
    while len(rows) > 1:
        odd = (group // step) % 2 == 1
        rows = [jnp.where(odd, rows[a + 1], rows[a]) for a in range(0, len(rows), 2)]
        step *= 2
    return rows[0]


def expand_section(src, src_at, dst, dst_at, count, emat):
    block = 256

    def step(i, carry):
        q = pl.multiple_of(i * block, block)
        high, low = split(src[pl.ds(src_at + q, block), :])
        wide = jnp.dot(
            jnp.concatenate([high, low], axis=1), emat[...], preferred_element_type=F32
        )
        for j in range(G):
            dst[pl.ds(dst_at + j * count + q, block), :] = wide[:, j * LANES : (j + 1) * LANES]
        return carry

    lax.fori_loop(0, count // block, step, 0)


def start_lists(source, lists, sems):
    copies = [
        pltpu.make_async_copy(source.at[k], lists[k], sems.at[k]) for k in range(len(lists))
    ]
    for copy in copies:
        copy.start()
    return copies


def setup_kernel(
    nmain, nface, first, second, face_row, face_hbm, raw, emat, out, face_send, slots, X, sems, *faces
):
    qmain, qface = nmain // G, nface // G
    copies = start_lists(face_hbm, faces, sems)
    hi_count = nmain // 128
    chunk = 1024
    table = jnp.zeros((256, hi_count), F32)
    for at in range(0, nface, chunk):
        node = face_row[:, at : at + chunk]
        pos = lax.broadcasted_iota(jnp.int32, (1, chunk), 1) + (at + 1)
        low = lax.broadcasted_iota(jnp.int32, (128, chunk), 0) == (node & 127)
        high = lax.broadcasted_iota(jnp.int32, (hi_count, chunk), 0) == (node >> 7)
        big = jnp.where(low, (pos >> 6).astype(F32), 0.0)
        small = jnp.where(low, (pos & 63).astype(F32), 0.0)
        table += lax.dot_general(
            jnp.concatenate([big, small], axis=0).astype(BF16),
            high.astype(F32).astype(BF16),
            (((1,), (1,)), ((), ())),
            preferred_element_type=F32,
        )
    table = table.astype(BF16)
    width = raw.shape[1]
    owned = (KU - 1) * G
    for k in range(owned):
        node = raw[k : k + 1, :]
        high = lax.broadcasted_iota(jnp.int32, (hi_count, width), 0) == (node >> 7)
        got = jnp.dot(table, high.astype(F32).astype(BF16), preferred_element_type=F32)
        both = got[:128] * 64.0 + got[128:]
        low = lax.broadcasted_iota(jnp.int32, (128, width), 0) == (node & 127)
        pos = jnp.sum(jnp.where(low, both, 0.0), axis=0, keepdims=True).astype(jnp.int32)
        slots[k : k + 1, :] = jnp.where(pos > 0, nmain + pos - 1, node)
    slots[owned:, :] = raw[owned:, :] + nface
    def turn(i, carry):
        q = pl.multiple_of(i * 128, 128)
        parts = []
        for j in range(G):
            parts.append(first[:, pl.ds(j * qmain + q, 128)])
            parts.append(second[:, pl.ds(j * qmain + q, 128)])
        out[pl.ds(q, 128), :] = jnp.concatenate(parts, axis=0).T
        return carry

    lax.fori_loop(0, qmain // 128, turn, 0)
    expand_section(out, 0, X, 0, qmain, emat)
    for copy in copies:
        copy.wait()
    zero = jnp.zeros((1, LANES), F32)

    def take(q, carry):
        nodes = [faces[j][q] for j in range(G)]
        out[pl.ds(qmain + q, 1), :] = merge_groups([X[pl.ds(n, 1), :] for n in nodes])
        for n in nodes:
            X[pl.ds(n, 1), :] = zero
        return carry

    lax.fori_loop(0, qface, take, 0, unroll=4)

    def pack(i, carry):
        q = pl.multiple_of(i * 8, 8)
        out[pl.ds(q, 8), :] = merge_groups([X[pl.ds(j * qmain + q, 8), :] for j in range(G)])
        return carry

    lax.fori_loop(0, qmain // 8, pack, 0, unroll=4)
    face_send[...] = out[qmain : qmain + qface, :].astype(BF16)


def setup(first, second, face_nodes, raw, emat):
    nmain, nface = first.shape[1], face_nodes.shape[0]
    qmain, qface = nmain // G, nface // G
    vmem = pl.BlockSpec(memory_space=pltpu.VMEM)
    return pl.pallas_call(
        functools.partial(setup_kernel, nmain, nface),
        name="setup_rows",
        out_shape=[
            jax.ShapeDtypeStruct((qmain + qface, LANES), F32),
            jax.ShapeDtypeStruct((qface, LANES), BF16),
            jax.ShapeDtypeStruct(raw.shape, jnp.int32),
        ],
        in_specs=[vmem, vmem, vmem, pl.BlockSpec(memory_space=pl.ANY), vmem, vmem],
        out_specs=[vmem, vmem, vmem],
        scratch_shapes=[
            pltpu.VMEM((nmain, LANES), F32),
            pltpu.SemaphoreType.DMA((G,)),
        ]
        + [pltpu.SMEM((qface,), jnp.int32)] * G,
        compiler_params=pltpu.CompilerParams(vmem_limit_bytes=VMEM_LIMIT),
    )(first, second, face_nodes.reshape(1, nface), face_nodes.reshape(G, qface), raw, emat)


def element_kernel(
    sections, chunks, steps, mainface, ghost, slots_hbm, mcat, kin, pot, emat, fmat,
    part, X, acc0, acc1, U, Y, sems, *lists,
):
    copies = start_lists(slots_hbm, lists, sems)
    accs = (acc0, acc1)
    at = 0
    src, src_at = mainface, 0
    for i, count in enumerate(sections):
        if i == 2:
            src, src_at = ghost, 0
        expand_section(src, src_at, X, at, count, emat)
        at += G * count
        src_at += count
    total = at
    zero = jnp.zeros((64, LANES), F32)

    def clear(i, carry):
        q = pl.multiple_of(i * 64, 64)
        acc0[pl.ds(q, 64), :] = zero
        acc1[pl.ds(q, 64), :] = zero
        return carry

    lax.fori_loop(0, total // 64, clear, 0)
    U[...] = jnp.zeros_like(U)
    for copy in copies:
        copy.wait()
    group = lane_group()
    masks = [group == j for j in range(G)]

    def gather(c, r):
        t = c * steps + r
        for b in range(KU):
            rows = [X[pl.ds(lists[b * G + j][t], 1), :] for j in range(G)]
            U[pl.ds(b * steps + r, 1), :] = merge_groups(rows)

    def scatter(c, r):
        t = c * steps + r
        for b in range(KU):
            acc = accs[b % 2]
            y = Y[pl.ds(b * steps + r, 1), :]
            nodes = [lists[b * G + j][t] for j in range(G)]
            sums = [acc[pl.ds(n, 1), :] + y for n in nodes]
            for j in range(G):
                pltpu.store(acc.at[pl.ds(nodes[j], 1), :], sums[j], mask=masks[j])

    def product(c):
        high, low = split(U[...])
        prod = jnp.dot(
            mcat[...], jnp.concatenate([high, high, low], axis=0), preferred_element_type=F32
        )
        Y[...] = kin[pl.ds(c, 1), :] * prod[:128] + pot[pl.ds(c, 1), :] * prod[128:]

    def first(r, carry):
        gather(0, r)
        return carry

    lax.fori_loop(0, steps, first, 0)

    def chunk(c, carry):
        product(c)

        def step(r, inner):
            gather(c + 1, r)
            scatter(c, r)
            return inner

        lax.fori_loop(0, steps, step, 0)
        return carry

    lax.fori_loop(0, chunks - 1, chunk, 0)
    product(chunks - 1)

    def last(r, carry):
        scatter(chunks - 1, r)
        return carry

    lax.fori_loop(0, steps, last, 0)
    at, out_at = 0, 0
    block = 256
    for count in sections:

        def fold(i, carry, at=at, out_at=out_at, count=count):
            q = pl.multiple_of(i * block, block)
            pieces = []
            for j in range(G):
                rows = pl.ds(at + j * count + q, block)
                pieces.extend(split(acc0[rows, :] + acc1[rows, :]))
            part[pl.ds(out_at + q, block), :] = jnp.dot(
                jnp.concatenate(pieces, axis=1), fmat[...], preferred_element_type=F32
            )
            return carry

        lax.fori_loop(0, count // block, fold, 0)
        at += G * count
        out_at += count


def elements(mainface, ghost, slots, mcat, kin, pot, emat, fmat, qmain, steps):
    qface = mainface.shape[0] - qmain
    sections = (qmain, qface, ghost.shape[0])
    total = sum(sections)
    chunks = kin.shape[0]
    vmem = pl.BlockSpec(memory_space=pltpu.VMEM)
    return pl.pallas_call(
        functools.partial(element_kernel, sections, chunks, steps),
        name="element_rows",
        out_shape=jax.ShapeDtypeStruct((total, LANES), F32),
        in_specs=[vmem, vmem, pl.BlockSpec(memory_space=pl.ANY)] + [vmem] * 5,
        out_specs=vmem,
        scratch_shapes=[
            pltpu.VMEM((G * total, LANES), F32),
            pltpu.VMEM((G * total, LANES), F32),
            pltpu.VMEM((G * total, LANES), F32),
            pltpu.VMEM((128, LANES), F32),
            pltpu.VMEM((128, LANES), F32),
            pltpu.SemaphoreType.DMA((KU * G,)),
        ]
        + [pltpu.SMEM((slots.shape[1],), jnp.int32)] * (KU * G),
        compiler_params=pltpu.CompilerParams(vmem_limit_bytes=VMEM_LIMIT),
    )(mainface, ghost, slots, mcat, kin, pot, emat, fmat)


def exchange_kernel(
    qmain, qface, parts, coef, part, cur, cur_ghost, prev, prev_ghost, out, out_ghost,
    own, theirs, new, new_ghost, up_send, down_send, from_below, from_above,
    load_sem, store_sem, send_sem, recv_sem, side_send, side_recv, relay_send, relay_recv,
):
    pieces = 4
    rows = qmain // pieces
    half = qface // 2
    space, state = lax.axis_index("space"), lax.axis_index("state")
    core = lax.rem(state, 2)
    other = state + 1 - 2 * core
    above = lax.rem(space + 1, parts)
    below = lax.rem(space + parts - 1, parts)
    load = pltpu.make_async_copy(part, own, load_sem)
    load.start()
    barrier = pltpu.get_barrier_semaphore()
    for device in ((space, other), (above, state), (below, state)):
        pl.semaphore_signal(barrier, inc=1, device_id=device, device_id_type=MESH)
    pl.semaphore_wait(barrier, 3)

    mine = pl.multiple_of(core * half, half)
    not_mine = pl.multiple_of((1 - core) * half, half)
    face_at, ghost_at = qmain, qmain + qface
    spans = (
        [pl.ds(face_at + not_mine, half), pl.ds(ghost_at + not_mine, half)]
        + [pl.ds(i * rows, rows) for i in range(pieces)]
        + [pl.ds(face_at + mine, half), pl.ds(ghost_at + mine, half)]
    )
    swaps = []
    for i, span in enumerate(spans):
        swap = pltpu.make_async_remote_copy(
            src_ref=part.at[span, :], dst_ref=theirs.at[span, :],
            send_sem=send_sem.at[i], recv_sem=recv_sem.at[i],
            device_id=(space, other), device_id_type=MESH,
        )
        swap.start()
        swaps.append(swap)

    def arrived(i, span):
        pltpu.make_async_remote_copy(
            src_ref=part.at[span, :], dst_ref=theirs.at[span, :],
            send_sem=send_sem.at[i], recv_sem=recv_sem.at[i],
            device_id=(space, other), device_id_type=MESH,
        ).wait_recv()

    load.wait()
    face_mine, ghost_mine = pl.ds(face_at + mine, half), pl.ds(ghost_at + mine, half)
    face_other, ghost_other = pl.ds(face_at + not_mine, half), pl.ds(ghost_at + not_mine, half)
    here, there = pl.ds(mine, half), pl.ds(not_mine, half)
    arrived(0, face_mine)
    down_send[...] = own[face_mine, :] + theirs[face_mine, :]
    arrived(1, ghost_mine)
    up_send[...] = own[ghost_mine, :] + theirs[ghost_mine, :]
    sides = []
    for i, (src, dst, place) in enumerate(
        ((up_send, from_below, above), (down_send, from_above, below))
    ):
        side = pltpu.make_async_remote_copy(
            src_ref=src, dst_ref=dst.at[here, :],
            send_sem=side_send.at[i], recv_sem=side_recv.at[i],
            device_id=(place, state), device_id_type=MESH,
        )
        side.start()
        sides.append(side)

    gain, damp, center = coef[0], coef[1], coef[2]

    def step(h, now, before):
        return (h - center * now) * gain - damp * before

    stores = []

    def keep(src, dst, span):
        copy = pltpu.make_async_copy(
            src.at[span, :], dst.at[span, :], store_sem.at[len(stores)]
        )
        copy.start()
        stores.append(copy)

    for i in range(pieces):
        span = spans[i + 2]
        swaps[i + 2].wait_recv()
        new[span, :] = step(own[span, :] + theirs[span, :], cur[span, :], prev[span, :])
        keep(new, out, span)
    arrived(6, face_other)
    arrived(7, ghost_other)
    relays = []
    for i, dst in enumerate((from_below, from_above)):
        sides[i].wait_recv()
        relay = pltpu.make_async_remote_copy(
            src_ref=dst.at[here, :], dst_ref=dst.at[here, :],
            send_sem=relay_send.at[i], recv_sem=relay_recv.at[i],
            device_id=(space, other), device_id_type=MESH,
        )
        relay.start()
        relays.append(relay)

    def finish(face_span, ghost_span, span):
        h = own[face_span, :] + theirs[face_span, :]
        extra = from_below[span, :]
        h = h + jnp.where(space == 0, jnp.zeros_like(extra), extra)
        new[face_span, :] = step(h, cur[face_span, :], prev[face_span, :])
        keep(new, out, face_span)
        h = own[ghost_span, :] + theirs[ghost_span, :] + from_above[span, :]
        h = jnp.where(space == parts - 1, jnp.zeros_like(h), h)
        new_ghost[span, :] = step(h, cur_ghost[span, :], prev_ghost[span, :])
        keep(new_ghost, out_ghost, span)

    finish(face_mine, ghost_mine, here)
    for i, dst in enumerate((from_below, from_above)):
        pltpu.make_async_remote_copy(
            src_ref=dst.at[there, :], dst_ref=dst.at[there, :],
            send_sem=relay_send.at[i], recv_sem=relay_recv.at[i],
            device_id=(space, other), device_id_type=MESH,
        ).wait_recv()
    finish(face_other, ghost_other, there)
    for copy in swaps + sides + relays:
        copy.wait_send()
    for copy in stores:
        copy.wait()


def exchange(coef, part, cur, cur_ghost, prev, prev_ghost, qmain):
    qface = cur_ghost.shape[0]
    parts = lax.axis_size("space")
    vmem = pl.BlockSpec(memory_space=pltpu.VMEM)
    hbm = pl.BlockSpec(memory_space=pltpu.HBM)
    half = qface // 2
    return pl.pallas_call(
        functools.partial(exchange_kernel, qmain, qface, parts),
        name="exchange_update",
        out_shape=[
            jax.ShapeDtypeStruct(cur.shape, F32),
            jax.ShapeDtypeStruct(cur_ghost.shape, F32),
        ],
        in_specs=[pl.BlockSpec(memory_space=pltpu.SMEM), hbm] + [vmem] * 4,
        out_specs=[hbm, hbm],
        scratch_shapes=[
            pltpu.VMEM(part.shape, F32),
            pltpu.VMEM(part.shape, F32),
            pltpu.VMEM(cur.shape, F32),
            pltpu.VMEM(cur_ghost.shape, F32),
            pltpu.VMEM((half, LANES), F32),
            pltpu.VMEM((half, LANES), F32),
            pltpu.VMEM((qface, LANES), F32),
            pltpu.VMEM((qface, LANES), F32),
            pltpu.SemaphoreType.DMA,
            pltpu.SemaphoreType.DMA((8,)),
            pltpu.SemaphoreType.DMA((8,)),
            pltpu.SemaphoreType.DMA((8,)),
            pltpu.SemaphoreType.DMA((2,)),
            pltpu.SemaphoreType.DMA((2,)),
            pltpu.SemaphoreType.DMA((2,)),
            pltpu.SemaphoreType.DMA((2,)),
        ],
        compiler_params=pltpu.CompilerParams(
            collective_id=0, has_side_effects=True, vmem_limit_bytes=32 * 2**20
        ),
    )(coef, part, cur, cur_ghost, prev, prev_ghost)


def margin_kernel(grid, node_total, rounded, out, blocks, gram, sums, across, along, *sems):
    depth, width, ring = grid
    space, state = lax.axis_index("space"), lax.axis_index("state")
    z, x = space // width, lax.rem(space, width)
    y, core = state // 2, lax.rem(state, 2)
    chips = ring // 2
    state_send, state_recv, row_send, row_recv, x_send, x_recv, z_send, z_recv = sems
    friends = [(space, lax.rem(state + k, ring)) for k in range(1, ring)]
    x_friends = [(z * width + lax.rem(x + k, width), state) for k in range(1, width)]
    z_friends = [(lax.rem(z + k, depth) * width + x, state) for k in range(1, depth)]
    barrier = pltpu.get_barrier_semaphore()
    everyone = friends + x_friends + z_friends
    for device in everyone:
        pl.semaphore_signal(barrier, inc=1, device_id=device, device_id_type=MESH)
    pl.semaphore_wait(barrier, len(everyone))

    copies = []
    for k in range(1, chips):
        to = lax.rem(y + k, chips)
        copy = pltpu.make_async_remote_copy(
            src_ref=rounded.at[to], dst_ref=blocks.at[k],
            send_sem=state_send.at[k], recv_sem=state_recv.at[k],
            device_id=(space, 2 * to + core), device_id_type=MESH,
        )
        copy.start()
        copies.append(copy)
    blocks[0] = rounded[y]
    for copy in copies:
        copy.wait()
    ordered = jnp.concatenate([blocks[lax.rem(y + chips - i, chips)] for i in range(chips)], axis=0)
    gram[:, : ordered.shape[0]] = lax.dot_general(
        ordered, ordered, (((1,), (1,)), ((), ())), preferred_element_type=F32
    )
    gram[:, ordered.shape[0] :] = jnp.zeros_like(gram[:, ordered.shape[0] :])

    def add_up(sources, friends, slots, send, recv):
        copies = []
        for k, (src, device) in enumerate(zip(sources, friends), 1):
            copy = pltpu.make_async_remote_copy(
                src_ref=src, dst_ref=slots.at[k], send_sem=send.at[k], recv_sem=recv.at[k],
                device_id=device, device_id_type=MESH,
            )
            copy.start()
            copies.append(copy)
        for copy in copies:
            copy.wait()
        return functools.reduce(lambda a, b: a + b, [slots[k] for k in range(1, len(friends) + 1)])

    def rows_of(member):
        return pl.ds(pl.multiple_of(member * 8, 8), 8)

    rows = [gram.at[rows_of(device[1]), :] for device in friends]
    total = gram[rows_of(state), :] + add_up(rows, friends, sums, row_send, row_recv)
    across[0] = total
    total = total + add_up([across.at[0]] * (width - 1), x_friends, across, x_send, x_recv)
    along[0] = total
    total = total + add_up([along.at[0]] * (depth - 1), z_friends, along, z_send, z_recv)
    out[...] = total[:, : out.shape[1]] * (1.0 / node_total)


def margin_of(rounded, node_total):
    ring = lax.axis_size("state")
    parts = lax.axis_size("space")
    width = 4
    depth = parts // width
    chips = ring // 2
    count = 8 * ring
    vmem = pl.BlockSpec(memory_space=pltpu.VMEM)
    sems = [pltpu.SemaphoreType.DMA((n,)) for n in (chips, chips, ring, ring, width, width, depth, depth)]
    return pl.pallas_call(
        functools.partial(margin_kernel, (depth, width, ring), node_total),
        name="margin_rows",
        out_shape=jax.ShapeDtypeStruct((8, count), F32),
        in_specs=[vmem],
        out_specs=vmem,
        scratch_shapes=[
            pltpu.VMEM(rounded.shape, BF16),
            pltpu.VMEM((count, LANES), F32),
            pltpu.VMEM((ring, 8, LANES), F32),
            pltpu.VMEM((width, 8, LANES), F32),
            pltpu.VMEM((depth, 8, LANES), F32),
        ]
        + sems,
        compiler_params=pltpu.CompilerParams(
            collective_id=1, has_side_effects=True, vmem_limit_bytes=32 * 2**20
        ),
    )(rounded)


def final_kernel(qmain, qface, core_ref, mainface, face_hbm, emat, out, rounded, X, R, sems, *faces):
    copies = start_lists(face_hbm, faces, sems)
    expand_section(mainface, 0, X, 0, qmain, emat)
    expand_section(mainface, qmain, R, 0, qface, emat)
    for copy in copies:
        copy.wait()

    def put(q, carry):
        for j in range(G):
            X[pl.ds(faces[j][q], 1), :] = R[pl.ds(j * qface + q, 1), :]
        return carry

    lax.fori_loop(0, qface, put, 0, unroll=4)
    core = core_ref[0]

    def turn(i, carry):
        q = pl.multiple_of(i * 128, 128)
        rows = merge_groups([X[pl.ds(j * qmain + q, 128), :] for j in range(G)]).T
        for j in range(G):
            a = rows[j * W : j * W + 8]
            b = rows[j * W + 8 : j * W + 16]
            out[:, pl.ds(j * qmain + q, 128)] = jnp.where(core == 0, a, b)
        far = G // 2
        for j in range(far):
            a = rows[j * W : (j + 1) * W]
            b = rows[(far + j) * W : (far + j + 1) * W]
            rounded[j, :, pl.ds(q, 128)] = jnp.where(core == 0, a, b).astype(BF16)
        return carry

    lax.fori_loop(0, qmain // 128, turn, 0)


def final(core, mainface, face_nodes, emat, qmain):
    qface = mainface.shape[0] - qmain
    vmem = pl.BlockSpec(memory_space=pltpu.VMEM)
    return pl.pallas_call(
        functools.partial(final_kernel, qmain, qface),
        name="final_block",
        out_shape=[
            jax.ShapeDtypeStruct((8, G * qmain), F32),
            jax.ShapeDtypeStruct((G // 2, W, qmain), BF16),
        ],
        in_specs=[
            pl.BlockSpec(memory_space=pltpu.SMEM), vmem, pl.BlockSpec(memory_space=pl.ANY), vmem
        ],
        out_specs=[vmem, vmem],
        scratch_shapes=[
            pltpu.VMEM((G * qmain, LANES), F32),
            pltpu.VMEM((G * qface, LANES), F32),
            pltpu.SemaphoreType.DMA((G,)),
        ]
        + [pltpu.SMEM((qface,), jnp.int32)] * G,
        compiler_params=pltpu.CompilerParams(vmem_limit_bytes=VMEM_LIMIT),
    )(core, mainface, face_nodes.reshape(G, qface), emat)


def body(states, bounds, element_matrix, elem_nodes, face_nodes, kinetic, potential, elem_count):
    parts = lax.axis_size("space")
    members = lax.axis_size("state")
    core = lax.rem(lax.axis_index("state"), 2)
    npe, slot_count = elem_nodes.shape
    half = slot_count // 2
    chunks = half // G
    steps = npe // KU
    qmain = states.shape[1] // G

    alive = (jnp.arange(slot_count, dtype=jnp.int32) < elem_count[0]).astype(F32)

    def lanes_of(scale):
        mine = lax.dynamic_slice(scale, (core * half,), (half,))
        return jnp.repeat(mine.reshape(G, chunks).T, W, axis=1)

    kin = lanes_of(0.5 * kinetic * alive)
    pot = lanes_of(potential * alive)
    mine = lax.dynamic_slice(elem_nodes, (0, core * half), (npe, half))
    raw = mine.reshape(KU, steps, G, chunks).transpose(0, 2, 3, 1).reshape(KU * G, chunks * steps)
    raw = jnp.pad(raw, ((0, 0), (0, (-raw.shape[1]) % 128)))
    matrix = jnp.pad(element_matrix.reshape(2, npe, npe), ((0, 0), (0, 128 - npe), (0, 128 - npe)))
    matrix = matrix.reshape(256, 128)
    high = lax.reduce_precision(matrix, 8, 7)
    low = matrix - high
    mcat = jnp.concatenate([high, low, high], axis=1).astype(BF16)
    emat, fmat = expand_matrix(), fold_matrix()

    lowest, lower, upper = bounds[0], bounds[1], bounds[2]
    half_width = (upper - lower) / 2.0
    center = (upper + lower) / 2.0
    sigma = half_width / (lowest - center)
    gamma = 2.0 / sigma
    coefs = [jnp.stack([sigma / half_width, jnp.zeros_like(sigma), center])]
    for _ in range(DEG - 1):
        following = 1.0 / (gamma - sigma)
        coefs.append(jnp.stack([2.0 * following / half_width, sigma * following, center]))
        sigma = following

    partner = lax.ppermute(states, "state", [(i, i ^ 1) for i in range(members)])
    first = jnp.where(core == 0, states, partner)
    second = jnp.where(core == 0, partner, states)
    cur, face_send, slots = setup(first, second, face_nodes, raw, emat)
    ghost = lax.ppermute(face_send, "space", [(i, i - 1) for i in range(1, parts)]).astype(F32)
    prev, prev_ghost = cur, ghost
    for k in range(DEG):
        part = elements(cur, ghost, slots, mcat, kin, pot, emat, fmat, qmain, steps)
        new, new_ghost = exchange(coefs[k], part, cur, ghost, prev, prev_ghost, qmain)
        prev, prev_ghost, cur, ghost = cur, ghost, new, new_ghost
    filtered, rounded = final(core.reshape(1), cur, face_nodes, emat, qmain)
    margin = margin_of(rounded, states.shape[1] * parts)
    return filtered, margin


def solution(mesh):
    in_specs = (
        P("state", "space"),
        P(),
        P(),
        P(None, "space"),
        P("space"),
        P("space"),
        P("space"),
        P("space"),
    )
    out_specs = (P("state", "space"), P("state", None))
    return jax.shard_map(body, mesh=mesh, in_specs=in_specs, out_specs=out_specs, check_vma=False)
```

time: 1500 us -> 309 us (0.21); the launches traced: 1480 us -> 308 us
  other arithmetic: 833 us -> 2.64 us
  local copies, waits for them, and re-layouts: 484 us -> 20.5 us
  Pallas kernels: 0 us -> 272 us
  blocking collectives: 61.2 us -> 0 us
  waiting for transfers between devices: 51.9 us -> 3.16 us
  starting transfers between devices: 22.5 us -> 4.62 us
    scatter-add x8 -> x0, other arithmetic: 826 us -> none  [the longest x4 707 us: hamiltonian(): jnp.zeros((width, owned_count + face_count), jnp.float32).at[:, elem_nodes]]
    gather x12 -> x0, local copies, waits for them, and re-layouts: 346 us -> none  [the longest x8 291 us: hamiltonian(): gathered = extended[:, elem_nodes]]
    pallas_call x0 -> x11, Pallas kernels: none -> 272 us  [the longest x4 168 us: elements(): pl.pallas_call(functools.partial(element_kernel, sections, chunks, steps)...]
    psum x1 -> x0, blocking collectives: 61.2 us -> none  [body(): margin = lax.psum(partial_rows, 'space') / node_total]
    add x8 -> x0, local copies, waits for them, and re-layouts: 39.3 us -> none  [hamiltonian(): kin_live * product[:, :corner_count] + pot_live * product[:, corner_count:]]
    all_gather x1 -> x0, waiting for transfers between devices: 39 us -> none  [body(): lax.all_gather(rounded, 'state', axis=0, tiled=True)]
    slice x8 -> x0, local copies, waits for them, and re-layouts: 29.6 us -> none  [the longest x4 22.9 us: hamiltonian(): return summed[:, :owned_count].at[:, face_nodes].add(returned)]
    scatter-add x4 -> x0, local copies, waits for them, and re-layouts: 22.2 us -> none  [hamiltonian(): return summed[:, :owned_count].at[:, face_nodes].add(returned)]
  transfers between devices with their start and end apart: 9 -> 2, of which waited for: 5 -> 1; matrix products, arithmetic and copies ran while one was open for 2% -> 3% of each run, Pallas kernels for 0% -> 0%
where the time goes in v1:
time: 309 us; the launch traced here: 308 us
  Pallas kernels  272 us (88%)
  local copies, waits for them, and re-layouts  20.5 us (7%)
  between operations  5.3 us (2%)
  starting transfers between devices  4.62 us (1%)
  waiting for transfers between devices  3.16 us (1%)
    pallas_call x4, Pallas kernels, elements(): pl.pallas_call(functools.partial(element_kernel, sections, chunks, steps)...  168 us
    pallas_call x4, Pallas kernels, exchange(): pl.pallas_call(functools.partial(exchange_kernel, qmain, qface, parts), n...  54 us
    pallas_call x1, Pallas kernels, margin_of(): pl.pallas_call(functools.partial(margin_kernel, (depth, width, ring), nod...  21 us
    pallas_call x1, Pallas kernels, setup(): pl.pallas_call(functools.partial(setup_kernel, nmain, nface), name='setup...  18.3 us
    unnamed x49, local copies, waits for them, and re-layouts  13.5 us
    pallas_call x1, Pallas kernels, final(): pl.pallas_call(functools.partial(final_kernel, qmain, qface), name='final...  10.3 us
  transfers between devices with their start and end apart: 2, of which 1 were waited for; matrix products, arithmetic and copies ran while one was open for 3% of the time, Pallas kernels for 0%

profile of v1, /device:TPU:1, one launch (start us, length us, event | category | flops | bytes accessed | tf_op | source)
XLA Modules:
  0.0 308.0 jit_solution(6088988920140117286)
XLA Ops:
  0.6 3.3 %collective-permute-start = (f32[8,16384]{1,0:T(8,128)}, f32[8,16384]{1,0:T(8,128)S(1)}, u32[]{:S(2)}, u32[]{:S(2)}) collective-permute-start(f32[8,16384]{1,0:T(8,128)} %param.10), channel_id=1, source_target_pairs={{0,1},{1,0},{2,3},{3,2},{4,5},{5,4},{6,7},{7,6},{8,9},{9,8},{10,11... | collective-permute-start | bytes 1572872 | tf_op jit(solution)/shard_map/ppermute | solution.py:640
  4.0 1.4 fusion.2
  9.7 1.3 reshape.48.face_hbm
  14.6 18.3 %setup_rows.1 = (f32[2560,128]{1,0:T(8,128)}, bf16[512,128]{1,0:T(8,128)(2,1)}, s32[40,512]{1,0:T(8,128)}) custom-call(f32[8,16384]{1,0:T(8,128)} %get-tuple-element.27.first, f32[8,16384]{1,0:T(8,128)} %get-tuple-element.26.second, s32[1,4096]{1,0:T(1,128)} %bitcast.22, s32[8,512]{1,0:T(8,128)} %reshape.48.face_hbm, s32[40,512]{1,0:T(8,128)} %pad.8.raw, ...), custom_call_target="tpu_custom_call" | custom-call | tf_op jit(solution)/shard_map/setup_rows/pallas_call | solution.py:153
  32.9 1.3 collective-permute-start.1
  36.9 3.2 %collective-permute-done.1 = bf16[512,128]{1,0:T(8,128)(2,1)S(1)} collective-permute-done((bf16[512,128]{1,0:T(8,128)(2,1)}, bf16[512,128]{1,0:T(8,128)(2,1)S(1)}, u32[]{:S(2)}, u32[]{:S(2)}) %collective-permute-start.1) | collective-permute-done | bytes 131104 | tf_op jit(solution)/shard_map/ppermute | solution.py:644
  40.8 42.2 %element_rows.4.part = f32[3072,128]{1,0:T(8,128)} custom-call(f32[2560,128]{1,0:T(8,128)} %get-tuple-element.14.mainface.cur.prev, f32[512,128]{1,0:T(8,128)} %convert_element_type.4.ghost.cur_ghost.prev_ghost, s32[40,512]{1,0:T(8,128)} %get-tuple-element.16.slots_hbm, bf16[256,384]{1,0:T(8,128)(2,1)} %pad_maximum_fusion.mcat, f32[16,128]{1,0:T(8,128)} %reshape.54.kin, ...), custom_call_target="tpu_custom_call" | custom-call | tf_op jit(solution)/shard_map/element_rows/pallas_call | solution.py:276
  83.0 1.4 copy-done.10
  84.4 14.9 %exchange_update.4 = (f32[2560,128]{1,0:T(8,128)S(1)}, f32[512,128]{1,0:T(8,128)S(1)}) custom-call(f32[3]{0:T(128)S(1)} %get-tuple-element.36.coef, f32[3072,128]{1,0:T(8,128)S(1)} %copy-done.10, f32[2560,128]{1,0:T(8,128)S(1)} %copy-done.1, f32[512,128]{1,0:T(8,128)S(1)} %copy-done.6, f32[2560,128]{1,0:T(8,128)S(1)} %copy-done.1, f32[512,128]{1,0:T(8,128)S(1)} %copy-done.6), custom_call_target="tpu_custom_call" | custom-call | tf_op jit(solution)/shard_map/exchange_update/pallas_call | solution.py:423
  99.3 1.0 copy-done.4
  101.1 42.0 %element_rows.5.part = f32[3072,128]{1,0:T(8,128)} custom-call(f32[2560,128]{1,0:T(8,128)} %copy-done.4, f32[512,128]{1,0:T(8,128)} %copy-done.15, s32[40,512]{1,0:T(8,128)} %get-tuple-element.16.slots_hbm, bf16[256,384]{1,0:T(8,128)(2,1)} %pad_maximum_fusion.mcat, f32[16,128]{1,0:T(8,128)} %reshape.54.kin, f32[16,128]{1,0:T(8,128)} %reshape.56.pot, ...), custom_call_target="tpu_custom_call" | custom-call | tf_op jit(solution)/shard_map/element_rows/pallas_call | solution.py:276
  143.1 1.4 copy-done.8
  144.5 13.1 %exchange_update.5 = (f32[2560,128]{1,0:T(8,128)S(1)}, f32[512,128]{1,0:T(8,128)S(1)}) custom-call(f32[3]{0:T(128)S(1)} %get-tuple-element.35.coef, f32[3072,128]{1,0:T(8,128)S(1)} %copy-done.8, f32[2560,128]{1,0:T(8,128)S(1)} %copy-done.5, f32[512,128]{1,0:T(8,128)S(1)} %copy-done.16, f32[2560,128]{1,0:T(8,128)S(1)} %copy-done.1, f32[512,128]{1,0:T(8,128)S(1)} %copy-done.6), custom_call_target="tpu_custom_call" | custom-call | tf_op jit(solution)/shard_map/exchange_update/pallas_call | solution.py:423
  157.6 1.0 copy-done.2
  159.4 42.0 %element_rows.6.part = f32[3072,128]{1,0:T(8,128)} custom-call(f32[2560,128]{1,0:T(8,128)} %copy-done.2, f32[512,128]{1,0:T(8,128)} %copy-done.13, s32[40,512]{1,0:T(8,128)} %get-tuple-element.16.slots_hbm, bf16[256,384]{1,0:T(8,128)(2,1)} %pad_maximum_fusion.mcat, f32[16,128]{1,0:T(8,128)} %reshape.54.kin, f32[16,128]{1,0:T(8,128)} %reshape.56.pot, ...), custom_call_target="tpu_custom_call" | custom-call | tf_op jit(solution)/shard_map/element_rows/pallas_call | solution.py:276
  201.4 1.4 copy-done.9
  202.8 12.8 %exchange_update.6 = (f32[2560,128]{1,0:T(8,128)S(1)}, f32[512,128]{1,0:T(8,128)S(1)}) custom-call(f32[3]{0:T(128)S(1)} %get-tuple-element.34.coef, f32[3072,128]{1,0:T(8,128)S(1)} %copy-done.9, f32[2560,128]{1,0:T(8,128)S(1)} %copy-done.3, f32[512,128]{1,0:T(8,128)S(1)} %copy-done.14, f32[2560,128]{1,0:T(8,128)S(1)} %copy-done.5, f32[512,128]{1,0:T(8,128)S(1)} %copy-done.16), custom_call_target="tpu_custom_call" | custom-call | tf_op jit(solution)/shard_map/exchange_update/pallas_call | solution.py:423
  215.7 1.0 copy-done.11
  217.4 42.0 %element_rows.7.part = f32[3072,128]{1,0:T(8,128)} custom-call(f32[2560,128]{1,0:T(8,128)} %copy-done.11, f32[512,128]{1,0:T(8,128)} %copy-done.18, s32[40,512]{1,0:T(8,128)} %get-tuple-element.16.slots_hbm, bf16[256,384]{1,0:T(8,128)(2,1)} %pad_maximum_fusion.mcat, f32[16,128]{1,0:T(8,128)} %reshape.54.kin, f32[16,128]{1,0:T(8,128)} %reshape.56.pot, ...), custom_call_target="tpu_custom_call" | custom-call | tf_op jit(solution)/shard_map/element_rows/pallas_call | solution.py:276
  259.4 1.4 copy-done.7
  260.8 13.2 %exchange_update.7 = (f32[2560,128]{1,0:T(8,128)S(1)}, f32[512,128]{1,0:T(8,128)}) custom-call(f32[3]{0:T(128)S(1)} %get-tuple-element.33.coef, f32[3072,128]{1,0:T(8,128)S(1)} %copy-done.7, f32[2560,128]{1,0:T(8,128)S(1)} %copy-done.12, f32[512,128]{1,0:T(8,128)S(1)} %copy-done.19, f32[2560,128]{1,0:T(8,128)S(1)} %copy-done.3, f32[512,128]{1,0:T(8,128)S(1)} %copy-done.14), custom_call_target="tpu_custom_call" | custom-call | tf_op jit(solution)/shard_map/exchange_update/pallas_call | solution.py:423
  274.0 1.1 copy-done.17
  275.1 10.3 %final_block.1 = (f32[8,16384]{1,0:T(8,128)}, bf16[4,16,2048]{2,1,0:T(8,128)(2,1)}) custom-call(s32[1]{0:T(128)} %bitcast.core_ref, f32[2560,128]{1,0:T(8,128)} %copy-done.17, s32[8,512]{1,0:T(8,128)} %reshape.48.face_hbm, bf16[256,1024]{1,0:T(8,128)(2,1)} %constant.35.clone.emat), custom_call_target="tpu_custom_call" | custom-call | tf_op jit(solution)/shard_map/final_block/pallas_call | solution.py:580
  286.4 21.0 %margin_rows.1 = f32[8,64]{1,0:T(8,128)S(1)} custom-call(bf16[4,16,2048]{2,1,0:T(8,128)(2,1)S(1)} %copy-done.20), custom_call_target="tpu_custom_call" | custom-call | tf_op jit(solution)/shard_map/margin_rows/pallas_call | solution.py:525
  (66 shorter events, 10.6 us)
Async XLA Ops:
  0.6 11.4 %copy-start = (s32[125,256]{1,0:T(8,128)S(1)}, s32[125,256]{1,0:T(8,128)}, u32[]{:S(2)}) copy-start(s32[125,256]{1,0:T(8,128)} %param.13) | copy-start | bytes 384004
  0.6 12.9 %collective-permute-start = (f32[8,16384]{1,0:T(8,128)}, f32[8,16384]{1,0:T(8,128)S(1)}, u32[]{:S(2)}, u32[]{:S(2)}) collective-permute-start(f32[8,16384]{1,0:T(8,128)} %param.10), channel_id=1, source_target_pairs={{0,1},{1,0},{2,3},{3,2},{4,5},{5,4},{6,7},{7,6},{8,9},{9,8},{10,11... | collective-permute-start | bytes 1572872 | tf_op jit(solution)/shard_map/ppermute | solution.py:640
  11.0 2.4 copy-start.22
  11.0 2.4 copy-start.23
  12.0 1.5 copy-start.21
  32.9 7.2 %collective-permute-start.1 = (bf16[512,128]{1,0:T(8,128)(2,1)}, bf16[512,128]{1,0:T(8,128)(2,1)S(1)}, u32[]{:S(2)}, u32[]{:S(2)}) collective-permute-start(bf16[512,128]{1,0:T(8,128)(2,1)} %get-tuple-element.15), channel_id=1, source_target_pairs={{8,0},{16,8},{24,16},{32,24},{40,32},{48,40},{56,48},{64,56},{72,6... | collective-permute-start | bytes 393224 | tf_op jit(solution)/shard_map/ppermute | solution.py:644
  40.8 42.2 %copy-start.1 = (f32[2560,128]{1,0:T(8,128)S(1)}, f32[2560,128]{1,0:T(8,128)}, u32[]{:S(2)}) copy-start(f32[2560,128]{1,0:T(8,128)} %get-tuple-element.14.mainface.cur.prev) | copy-start | bytes 3932164
  40.8 42.2 %copy-start.6 = (f32[512,128]{1,0:T(8,128)S(1)}, f32[512,128]{1,0:T(8,128)}, u32[]{:S(2)}) copy-start(f32[512,128]{1,0:T(8,128)} %convert_element_type.4.ghost.cur_ghost.prev_ghost) | copy-start | bytes 786436
  83.0 1.4 copy-start.10
  99.3 1.1 copy-start.4
  100.4 0.7 copy-start.15
  101.1 42.0 %copy-start.5 = (f32[2560,128]{1,0:T(8,128)S(1)}, f32[2560,128]{1,0:T(8,128)}, u32[]{:S(2)}) copy-start(f32[2560,128]{1,0:T(8,128)} %copy-done.4) | copy-start | bytes 3932164
  101.1 42.0 %copy-start.16 = (f32[512,128]{1,0:T(8,128)S(1)}, f32[512,128]{1,0:T(8,128)}, u32[]{:S(2)}) copy-start(f32[512,128]{1,0:T(8,128)} %copy-done.15) | copy-start | bytes 786436
  143.1 1.4 copy-start.8
  157.6 1.1 copy-start.2
  159.4 42.0 %copy-start.3 = (f32[2560,128]{1,0:T(8,128)S(1)}, f32[2560,128]{1,0:T(8,128)}, u32[]{:S(2)}) copy-start(f32[2560,128]{1,0:T(8,128)} %copy-done.2) | copy-start | bytes 3932164
  159.4 42.0 %copy-start.14 = (f32[512,128]{1,0:T(8,128)S(1)}, f32[512,128]{1,0:T(8,128)}, u32[]{:S(2)}) copy-start(f32[512,128]{1,0:T(8,128)} %copy-done.13) | copy-start | bytes 786436
  201.4 1.4 copy-start.9
  215.7 1.1 copy-start.11
  217.4 42.0 %copy-start.12 = (f32[2560,128]{1,0:T(8,128)S(1)}, f32[2560,128]{1,0:T(8,128)}, u32[]{:S(2)}) copy-start(f32[2560,128]{1,0:T(8,128)} %copy-done.11) | copy-start | bytes 3932164
  217.4 42.0 %copy-start.19 = (f32[512,128]{1,0:T(8,128)S(1)}, f32[512,128]{1,0:T(8,128)}, u32[]{:S(2)}) copy-start(f32[512,128]{1,0:T(8,128)} %copy-done.18) | copy-start | bytes 786436
  259.4 1.4 copy-start.7
  274.0 1.1 copy-start.17
  285.4 1.0 copy-start.20
  (2 other events, 1.4 us)

commit v2 on v1

--- a/solution.py
+++ b/solution.py
@@ -12,6 +12,7 @@
 G = 8
 W = 16
 LANES = G * W
+FACE_LIST = 1024
 KU = 5
 MESH = pl.DeviceIdType.MESH
 F32 = jnp.float32
@@ -41,22 +42,25 @@
     return high, low
 
 
-def lane_group():
-    return lax.broadcasted_iota(jnp.int32, (1, LANES), 1) // W
+def lane_group(rows=1):
+    return lax.broadcasted_iota(jnp.int32, (rows, LANES), 1) // W
+
+
+def odd_groups(rows, step):
+    return (lane_group(rows) & step) != 0
 
 
 def merge_groups(rows):
     step = 1
-    group = lane_group()
     while len(rows) > 1:
-        odd = (group // step) % 2 == 1
+        odd = odd_groups(rows[0].shape[0], step)
         rows = [jnp.where(odd, rows[a + 1], rows[a]) for a in range(0, len(rows), 2)]
         step *= 2
     return rows[0]
 
 
-def expand_section(src, src_at, dst, dst_at, count, emat):
-    block = 256
+def expand_section(src, src_at, dst, dst_at, count, emat, block=512, also=None):
+    block = min(block, count)
 
     def step(i, carry):
         q = pl.multiple_of(i * block, block)
@@ -66,6 +70,8 @@
         )
         for j in range(G):
             dst[pl.ds(dst_at + j * count + q, block), :] = wide[:, j * LANES : (j + 1) * LANES]
+        if also is not None:
+            also(dst_at + i * block * G, block * G)
         return carry
 
     lax.fori_loop(0, count // block, step, 0)
@@ -80,16 +86,35 @@
     return copies
 
 
+def start_faces(source, lists, sems):
+    size = lists[0].shape[0]
+    copies = [
+        pltpu.make_async_copy(source.at[pl.ds(k * size, size)], lists[k], sems.at[k])
+        for k in range(len(lists))
+    ]
+    for copy in copies:
+        copy.start()
+    return copies
+
+
+def faces_at(lists, count, q):
+    inside = lists[0].shape[0] // count
+    spots = [q + i * count for i in range(inside)]
+    return [lists[j // inside][spots[j % inside]] for j in range(G)]
+
+
 def setup_kernel(
-    nmain, nface, first, second, face_row, face_hbm, raw, emat, out, face_send, slots, X, sems, *faces
+    nmain, nface, first, second, face_row, face_hbm, raw, emat, out, face_high, face_low, slots, X, sems, *faces
 ):
     qmain, qface = nmain // G, nface // G
-    copies = start_lists(face_hbm, faces, sems)
+    copies = start_faces(face_hbm, faces, sems)
     hi_count = nmain // 128
     chunk = 1024
     table = jnp.zeros((256, hi_count), F32)
     for at in range(0, nface, chunk):
-        node = face_row[:, at : at + chunk]
+        node = jnp.concatenate(
+            [face_row[r : r + 1, :] for r in range(at // 128, (at + chunk) // 128)], axis=1
+        )
         pos = lax.broadcasted_iota(jnp.int32, (1, chunk), 1) + (at + 1)
         low = lax.broadcasted_iota(jnp.int32, (128, chunk), 0) == (node & 127)
         high = lax.broadcasted_iota(jnp.int32, (hi_count, chunk), 0) == (node >> 7)
@@ -129,7 +154,7 @@
     zero = jnp.zeros((1, LANES), F32)
 
     def take(q, carry):
-        nodes = [faces[j][q] for j in range(G)]
+        nodes = faces_at(faces, qface, q)
         out[pl.ds(qmain + q, 1), :] = merge_groups([X[pl.ds(n, 1), :] for n in nodes])
         for n in nodes:
             X[pl.ds(n, 1), :] = zero
@@ -143,7 +168,7 @@
         return carry
 
     lax.fori_loop(0, qmain // 8, pack, 0, unroll=4)
-    face_send[...] = out[qmain : qmain + qface, :].astype(BF16)
+    face_high[...], face_low[...] = split(out[qmain : qmain + qface, :])
 
 
 def setup(first, second, face_nodes, raw, emat):
@@ -156,17 +181,18 @@
         out_shape=[
             jax.ShapeDtypeStruct((qmain + qface, LANES), F32),
             jax.ShapeDtypeStruct((qface, LANES), BF16),
+            jax.ShapeDtypeStruct((qface, LANES), BF16),
             jax.ShapeDtypeStruct(raw.shape, jnp.int32),
         ],
         in_specs=[vmem, vmem, vmem, pl.BlockSpec(memory_space=pl.ANY), vmem, vmem],
-        out_specs=[vmem, vmem, vmem],
+        out_specs=[vmem, vmem, vmem, vmem],
         scratch_shapes=[
             pltpu.VMEM((nmain, LANES), F32),
-            pltpu.SemaphoreType.DMA((G,)),
+            pltpu.SemaphoreType.DMA((G * qface // FACE_LIST,)),
         ]
-        + [pltpu.SMEM((qface,), jnp.int32)] * G,
+        + [pltpu.SMEM((FACE_LIST,), jnp.int32)] * (G * qface // FACE_LIST),
         compiler_params=pltpu.CompilerParams(vmem_limit_bytes=VMEM_LIMIT),
-    )(first, second, face_nodes.reshape(1, nface), face_nodes.reshape(G, qface), raw, emat)
+    )(first, second, face_nodes.reshape(nface // 128, 128), face_nodes, raw, emat)
 
 
 def element_kernel(
@@ -175,83 +201,78 @@
 ):
     copies = start_lists(slots_hbm, lists, sems)
     accs = (acc0, acc1)
+
+    def clear(row, count):
+        row = pl.multiple_of(row, count)
+        zero = jnp.zeros((count, LANES), F32)
+        acc0[pl.ds(row, count), :] = zero
+        acc1[pl.ds(row, count), :] = zero
+
     at = 0
     src, src_at = mainface, 0
     for i, count in enumerate(sections):
         if i == 2:
             src, src_at = ghost, 0
-        expand_section(src, src_at, X, at, count, emat)
+        expand_section(src, src_at, X, at, count, emat, also=clear)
         at += G * count
         src_at += count
-    total = at
-    zero = jnp.zeros((64, LANES), F32)
-
-    def clear(i, carry):
-        q = pl.multiple_of(i * 64, 64)
-        acc0[pl.ds(q, 64), :] = zero
-        acc1[pl.ds(q, 64), :] = zero
-        return carry
-
-    lax.fori_loop(0, total // 64, clear, 0)
-    U[...] = jnp.zeros_like(U)
+    U[:, U.shape[1] - 8 :, :] = jnp.zeros((2, 8, LANES), F32)
     for copy in copies:
         copy.wait()
     group = lane_group()
     masks = [group == j for j in range(G)]
 
-    def gather(c, r):
-        t = c * steps + r
+    def gather(c, half, r):
+        t = (2 * c + half) * steps + r
         for b in range(KU):
             rows = [X[pl.ds(lists[b * G + j][t], 1), :] for j in range(G)]
-            U[pl.ds(b * steps + r, 1), :] = merge_groups(rows)
-
-    def scatter(c, r):
-        t = c * steps + r
+            U[half, pl.ds(b * steps + r, 1), :] = merge_groups(rows)
+
+    def scatter(c, half, r):
+        t = (2 * c + half) * steps + r
         for b in range(KU):
             acc = accs[b % 2]
-            y = Y[pl.ds(b * steps + r, 1), :]
+            y = Y[half, pl.ds(b * steps + r, 1), :]
             nodes = [lists[b * G + j][t] for j in range(G)]
             sums = [acc[pl.ds(n, 1), :] + y for n in nodes]
             for j in range(G):
                 pltpu.store(acc.at[pl.ds(nodes[j], 1), :], sums[j], mask=masks[j])
 
     def product(c):
-        high, low = split(U[...])
+        high, low = split(jnp.concatenate([U[0], U[1]], axis=1))
         prod = jnp.dot(
             mcat[...], jnp.concatenate([high, high, low], axis=0), preferred_element_type=F32
         )
-        Y[...] = kin[pl.ds(c, 1), :] * prod[:128] + pot[pl.ds(c, 1), :] * prod[128:]
-
-    def first(r, carry):
-        gather(0, r)
-        return carry
-
-    lax.fori_loop(0, steps, first, 0)
+        for half in range(2):
+            lanes = slice(half * LANES, (half + 1) * LANES)
+            row = pl.ds(2 * c + half, 1)
+            Y[half] = kin[row, :] * prod[:128, lanes] + pot[row, :] * prod[128:, lanes]
+
+    def loop(*works):
+        def step(r, carry):
+            for half in range(2):
+                for work, c in works:
+                    work(c, half, r)
+            return carry
+
+        lax.fori_loop(0, steps, step, 0, unroll=KU)
+
+    loop((gather, 0))
 
     def chunk(c, carry):
         product(c)
-
-        def step(r, inner):
-            gather(c + 1, r)
-            scatter(c, r)
-            return inner
-
-        lax.fori_loop(0, steps, step, 0)
+        loop((gather, c + 1), (scatter, c))
         return carry
 
-    lax.fori_loop(0, chunks - 1, chunk, 0)
-    product(chunks - 1)
-
-    def last(r, carry):
-        scatter(chunks - 1, r)
-        return carry
-
-    lax.fori_loop(0, steps, last, 0)
+    pairs = chunks // 2
+    lax.fori_loop(0, pairs - 1, chunk, 0)
+    product(pairs - 1)
+    loop((scatter, pairs - 1))
     at, out_at = 0, 0
-    block = 256
     for count in sections:
-
-        def fold(i, carry, at=at, out_at=out_at, count=count):
+        block = min(count, 512)
+
+        def fold(i, carry, at=at, out_at=out_at, count=count, block=block):
             q = pl.multiple_of(i * block, block)
             pieces = []
             for j in range(G):
@@ -279,22 +300,17 @@
         out_shape=jax.ShapeDtypeStruct((total, LANES), F32),
         in_specs=[vmem, vmem, pl.BlockSpec(memory_space=pl.ANY)] + [vmem] * 5,
         out_specs=vmem,
-        scratch_shapes=[
-            pltpu.VMEM((G * total, LANES), F32),
-            pltpu.VMEM((G * total, LANES), F32),
-            pltpu.VMEM((G * total, LANES), F32),
-            pltpu.VMEM((128, LANES), F32),
-            pltpu.VMEM((128, LANES), F32),
-            pltpu.SemaphoreType.DMA((KU * G,)),
-        ]
+        scratch_shapes=[pltpu.VMEM((G * total, LANES), F32)] * 3
+        + [pltpu.VMEM((2, 128, LANES), F32)] * 2
+        + [pltpu.SemaphoreType.DMA((KU * G,))]
         + [pltpu.SMEM((slots.shape[1],), jnp.int32)] * (KU * G),
         compiler_params=pltpu.CompilerParams(vmem_limit_bytes=VMEM_LIMIT),
     )(mainface, ghost, slots, mcat, kin, pot, emat, fmat)
 
 
 def exchange_kernel(
-    qmain, qface, parts, coef, part, cur, cur_ghost, prev, prev_ghost, out, out_ghost,
-    own, theirs, new, new_ghost, up_send, down_send, from_below, from_above,
+    qmain, qface, parts, coef, part, cur_in, cur_ghost_in, prev_in, prev_ghost_in, out, out_ghost,
+    own, cur, cur_ghost, prev, prev_ghost, theirs, new, new_ghost, up_send, down_send, from_below, from_above,
     load_sem, store_sem, send_sem, recv_sem, side_send, side_recv, relay_send, relay_recv,
 ):
     pieces = 4
@@ -305,8 +321,13 @@
     other = state + 1 - 2 * core
     above = lax.rem(space + 1, parts)
     below = lax.rem(space + parts - 1, parts)
-    load = pltpu.make_async_copy(part, own, load_sem)
-    load.start()
+    loads = []
+    for src, dst in (
+        (part, own), (cur_in, cur), (prev_in, prev), (cur_ghost_in, cur_ghost), (prev_ghost_in, prev_ghost)
+    ):
+        load = pltpu.make_async_copy(src, dst, load_sem.at[len(loads)])
+        load.start()
+        loads.append(load)
     barrier = pltpu.get_barrier_semaphore()
     for device in ((space, other), (above, state), (below, state)):
         pl.semaphore_signal(barrier, inc=1, device_id=device, device_id_type=MESH)
@@ -337,14 +358,15 @@
             device_id=(space, other), device_id_type=MESH,
         ).wait_recv()
 
-    load.wait()
+    for load in loads:
+        load.wait()
     face_mine, ghost_mine = pl.ds(face_at + mine, half), pl.ds(ghost_at + mine, half)
     face_other, ghost_other = pl.ds(face_at + not_mine, half), pl.ds(ghost_at + not_mine, half)
     here, there = pl.ds(mine, half), pl.ds(not_mine, half)
     arrived(0, face_mine)
-    down_send[...] = own[face_mine, :] + theirs[face_mine, :]
+    down_send[...] = (own[face_mine, :] + theirs[face_mine, :]).astype(BF16)
     arrived(1, ghost_mine)
-    up_send[...] = own[ghost_mine, :] + theirs[ghost_mine, :]
+    up_send[...] = (own[ghost_mine, :] + theirs[ghost_mine, :]).astype(BF16)
     sides = []
     for i, (src, dst, place) in enumerate(
         ((up_send, from_below, above), (down_send, from_above, below))
@@ -391,11 +413,11 @@
 
     def finish(face_span, ghost_span, span):
         h = own[face_span, :] + theirs[face_span, :]
-        extra = from_below[span, :]
+        extra = from_below[span, :].astype(F32)
         h = h + jnp.where(space == 0, jnp.zeros_like(extra), extra)
         new[face_span, :] = step(h, cur[face_span, :], prev[face_span, :])
         keep(new, out, face_span)
-        h = own[ghost_span, :] + theirs[ghost_span, :] + from_above[span, :]
+        h = own[ghost_span, :] + theirs[ghost_span, :] + from_above[span, :].astype(F32)
         h = jnp.where(space == parts - 1, jnp.zeros_like(h), h)
         new_ghost[span, :] = step(h, cur_ghost[span, :], prev_ghost[span, :])
         keep(new_ghost, out_ghost, span)
@@ -417,7 +439,6 @@
 def exchange(coef, part, cur, cur_ghost, prev, prev_ghost, qmain):
     qface = cur_ghost.shape[0]
     parts = lax.axis_size("space")
-    vmem = pl.BlockSpec(memory_space=pltpu.VMEM)
     hbm = pl.BlockSpec(memory_space=pltpu.HBM)
     half = qface // 2
     return pl.pallas_call(
@@ -427,18 +448,22 @@
             jax.ShapeDtypeStruct(cur.shape, F32),
             jax.ShapeDtypeStruct(cur_ghost.shape, F32),
         ],
-        in_specs=[pl.BlockSpec(memory_space=pltpu.SMEM), hbm] + [vmem] * 4,
+        in_specs=[pl.BlockSpec(memory_space=pltpu.SMEM)] + [hbm] * 5,
         out_specs=[hbm, hbm],
         scratch_shapes=[
             pltpu.VMEM(part.shape, F32),
+            pltpu.VMEM(cur.shape, F32),
+            pltpu.VMEM(cur_ghost.shape, F32),
+            pltpu.VMEM(cur.shape, F32),
+            pltpu.VMEM(cur_ghost.shape, F32),
             pltpu.VMEM(part.shape, F32),
             pltpu.VMEM(cur.shape, F32),
             pltpu.VMEM(cur_ghost.shape, F32),
-            pltpu.VMEM((half, LANES), F32),
-            pltpu.VMEM((half, LANES), F32),
-            pltpu.VMEM((qface, LANES), F32),
-            pltpu.VMEM((qface, LANES), F32),
-            pltpu.SemaphoreType.DMA,
+            pltpu.VMEM((half, LANES), BF16),
+            pltpu.VMEM((half, LANES), BF16),
+            pltpu.VMEM((qface, LANES), BF16),
+            pltpu.VMEM((qface, LANES), BF16),
+            pltpu.SemaphoreType.DMA((5,)),
             pltpu.SemaphoreType.DMA((8,)),
             pltpu.SemaphoreType.DMA((8,)),
             pltpu.SemaphoreType.DMA((8,)),
@@ -448,7 +473,7 @@
             pltpu.SemaphoreType.DMA((2,)),
         ],
         compiler_params=pltpu.CompilerParams(
-            collective_id=0, has_side_effects=True, vmem_limit_bytes=32 * 2**20
+            collective_id=0, has_side_effects=True, vmem_limit_bytes=VMEM_LIMIT
         ),
     )(coef, part, cur, cur_ghost, prev, prev_ghost)
 
@@ -537,21 +562,21 @@
         ]
         + sems,
         compiler_params=pltpu.CompilerParams(
-            collective_id=1, has_side_effects=True, vmem_limit_bytes=32 * 2**20
+            collective_id=1, has_side_effects=True, vmem_limit_bytes=VMEM_LIMIT
         ),
     )(rounded)
 
 
 def final_kernel(qmain, qface, core_ref, mainface, face_hbm, emat, out, rounded, X, R, sems, *faces):
-    copies = start_lists(face_hbm, faces, sems)
+    copies = start_faces(face_hbm, faces, sems)
     expand_section(mainface, 0, X, 0, qmain, emat)
     expand_section(mainface, qmain, R, 0, qface, emat)
     for copy in copies:
         copy.wait()
 
     def put(q, carry):
-        for j in range(G):
-            X[pl.ds(faces[j][q], 1), :] = R[pl.ds(j * qface + q, 1), :]
+        for j, n in enumerate(faces_at(faces, qface, q)):
+            X[pl.ds(n, 1), :] = R[pl.ds(j * qface + q, 1), :]
         return carry
 
     lax.fori_loop(0, qface, put, 0, unroll=4)
@@ -591,11 +616,11 @@
         scratch_shapes=[
             pltpu.VMEM((G * qmain, LANES), F32),
             pltpu.VMEM((G * qface, LANES), F32),
-            pltpu.SemaphoreType.DMA((G,)),
+            pltpu.SemaphoreType.DMA((G * qface // FACE_LIST,)),
         ]
-        + [pltpu.SMEM((qface,), jnp.int32)] * G,
+        + [pltpu.SMEM((FACE_LIST,), jnp.int32)] * (G * qface // FACE_LIST),
         compiler_params=pltpu.CompilerParams(vmem_limit_bytes=VMEM_LIMIT),
-    )(core, mainface, face_nodes.reshape(G, qface), emat)
+    )(core, mainface, face_nodes, emat)
 
 
 def body(states, bounds, element_matrix, elem_nodes, face_nodes, kinetic, potential, elem_count):
@@ -640,13 +665,17 @@
     partner = lax.ppermute(states, "state", [(i, i ^ 1) for i in range(members)])
     first = jnp.where(core == 0, states, partner)
     second = jnp.where(core == 0, partner, states)
-    cur, face_send, slots = setup(first, second, face_nodes, raw, emat)
-    ghost = lax.ppermute(face_send, "space", [(i, i - 1) for i in range(1, parts)]).astype(F32)
-    prev, prev_ghost = cur, ghost
+    cur, face_high, face_low, slots = setup(first, second, face_nodes, raw, emat)
+    downwards = [(i, i - 1) for i in range(1, parts)]
+    ghost_high = lax.ppermute(face_high, "space", downwards).astype(F32)
+    ghost_low = lax.ppermute(face_low, "space", downwards).astype(F32)
+    prev, prev_ghost = cur, ghost_high + ghost_low
     for k in range(DEG):
+        ghost = new_ghost if k else ghost_high
         part = elements(cur, ghost, slots, mcat, kin, pot, emat, fmat, qmain, steps)
-        new, new_ghost = exchange(coefs[k], part, cur, ghost, prev, prev_ghost, qmain)
-        prev, prev_ghost, cur, ghost = cur, ghost, new, new_ghost
+        cur_ghost = ghost if k else prev_ghost
+        new, new_ghost = exchange(coefs[k], part, cur, cur_ghost, prev, prev_ghost, qmain)
+        prev, prev_ghost, cur = cur, cur_ghost, new
     filtered, rounded = final(core.reshape(1), cur, face_nodes, emat, qmain)
     margin = margin_of(rounded, states.shape[1] * parts)
     return filtered, margin

time: 309 us -> 261 us (0.84)
  Pallas kernels: 272 us -> 236 us
  local copies, waits for them, and re-layouts: 20.5 us -> 6.99 us
    pallas_call x4, Pallas kernels: 168 us -> 136 us  [elements(): pl.pallas_call(functools.partial(element_kernel, sections, chunks, steps)...]
    unnamed x49 -> x9, local copies, waits for them, and re-layouts: 13.5 us -> 1.3 us
  transfers between devices with their start and end apart: 2 -> 3, of which waited for: 1 -> 1; matrix products, arithmetic and copies ran while one was open for 3% -> 3% of each run, Pallas kernels for 0% -> 13%
where the time goes in v2:
time: 261 us; the launch traced here: 260 us
  Pallas kernels  236 us (90%)
  local copies, waits for them, and re-layouts  6.99 us (3%)
  starting transfers between devices  5.91 us (2%)
  between operations  5.2 us (2%)
  other arithmetic  4.56 us (2%)
    pallas_call x4, Pallas kernels, elements(): pl.pallas_call(functools.partial(element_kernel, sections, chunks, steps)...  136 us
    pallas_call x4, Pallas kernels, exchange(): pl.pallas_call(functools.partial(exchange_kernel, qmain, qface, parts), n...  51.2 us
    pallas_call x1, Pallas kernels, margin_of(): pl.pallas_call(functools.partial(margin_kernel, (depth, width, ring), nod...  22.4 us
    pallas_call x1, Pallas kernels, setup(): pl.pallas_call(functools.partial(setup_kernel, nmain, nface), name='setup...  17.6 us
    pallas_call x1, Pallas kernels, final(): pl.pallas_call(functools.partial(final_kernel, qmain, qface), name='final...  9.37 us
  transfers between devices with their start and end apart: 3, of which 1 were waited for; matrix products, arithmetic and copies ran while one was open for 3% of the time, Pallas kernels for 13%

profile of v2, /device:TPU:1, one launch (start us, length us, event | category | flops | bytes accessed | tf_op | source)
XLA Modules:
  0.0 260.2 jit_solution(10347630780500101459)
XLA Ops:
  0.6 3.3 %collective-permute-start = (f32[8,16384]{1,0:T(8,128)}, f32[8,16384]{1,0:T(8,128)S(1)}, u32[]{:S(2)}, u32[]{:S(2)}) collective-permute-start(f32[8,16384]{1,0:T(8,128)} %param.10), channel_id=1, source_target_pairs={{0,1},{1,0},{2,3},{3,2},{4,5},{5,4},{6,7},{7,6},{8,9},{9,8},{10,11... | collective-permute-start | bytes 1572872 | tf_op jit(solution)/shard_map/ppermute | solution.py:665
  4.0 1.4 fusion.2
  9.8 0.9 reshape.46
  12.8 1.1 broadcast_select_fusion
  13.9 17.6 %setup_rows.1 = (f32[2560,128]{1,0:T(8,128)}, bf16[512,128]{1,0:T(8,128)(2,1)}, bf16[512,128]{1,0:T(8,128)(2,1)}, s32[40,512]{1,0:T(8,128)}) custom-call(f32[8,16384]{1,0:T(8,128)} %get-tuple-element.29.first, f32[8,16384]{1,0:T(8,128)} %get-tuple-element.28.second, s32[32,128]{1,0:T(8,128)} %bitcast.22, s32[4096]{0:T(1024)} %face_hbm.3, s32[40,512]{1,0:T(8,128)} %pad.8.raw, ...), custom_call_target="tpu_custom_call" | custom-call | tf_op jit(solution)/shard_map/setup_rows/pallas_call | solution.py:178
  31.5 1.3 collective-permute-start.1
  32.8 1.3 collective-permute-start.2
  35.3 0.7 reshape.51.pot
  36.1 0.7 reshape.49.kin
  36.8 0.7 pad_maximum_fusion.mcat
  37.4 1.2 collective-permute-done.1
  38.7 0.7 convert_element_type.10.ghost
  39.4 34.0 %element_rows.4.part = f32[3072,128]{1,0:T(8,128)} custom-call(f32[2560,128]{1,0:T(8,128)} %get-tuple-element.15.mainface.cur_in.prev_in, f32[512,128]{1,0:T(8,128)} %convert_element_type.10.ghost, s32[40,512]{1,0:T(8,128)} %get-tuple-element.17.slots_hbm, bf16[256,384]{1,0:T(8,128)(2,1)} %pad_maximum_fusion.mcat, f32[16,128]{1,0:T(8,128)} %reshape.49.kin, ...), custom_call_target="tpu_custom_call" | custom-call | tf_op jit(solution)/shard_map/element_rows/pallas_call | solution.py:297
  73.4 0.7 convert_add_fusion.cur_ghost_in.prev_ghost_in
  74.2 15.0 %exchange_update.4 = (f32[2560,128]{1,0:T(8,128)}, f32[512,128]{1,0:T(8,128)}) custom-call(f32[3]{0:T(128)} %get-tuple-element.38.coef, f32[3072,128]{1,0:T(8,128)} %element_rows.4.part, f32[2560,128]{1,0:T(8,128)} %get-tuple-element.15.mainface.cur_in.prev_in, f32[512,128]{1,0:T(8,128)} %convert_add_fusion.cur_ghost_in.prev_ghost_in, ...), custom_call_target="tpu_custom_call" | custom-call | tf_op jit(solution)/shard_map/exchange_update/pallas_call | solution.py:444
  89.2 33.8 %element_rows.5.part = f32[3072,128]{1,0:T(8,128)} custom-call(f32[2560,128]{1,0:T(8,128)} %get-tuple-element.19.mainface.cur_in.prev_in, f32[512,128]{1,0:T(8,128)} %get-tuple-element.20.ghost.cur_ghost_in.prev_ghost_in, s32[40,512]{1,0:T(8,128)} %get-tuple-element.17.slots_hbm, bf16[256,384]{1,0:T(8,128)(2,1)} %pad_maximum_fusion.mcat, ...), custom_call_target="tpu_custom_call" | custom-call | tf_op jit(solution)/shard_map/element_rows/pallas_call | solution.py:297
  123.0 12.0 %exchange_update.5 = (f32[2560,128]{1,0:T(8,128)}, f32[512,128]{1,0:T(8,128)}) custom-call(f32[3]{0:T(128)} %get-tuple-element.37.coef, f32[3072,128]{1,0:T(8,128)} %element_rows.5.part, f32[2560,128]{1,0:T(8,128)} %get-tuple-element.19.mainface.cur_in.prev_in, f32[512,128]{1,0:T(8,128)} %get-tuple-element.20.ghost.cur_ghost_in.prev_ghost_in, ...), custom_call_target="tpu_custom_call" | custom-call | tf_op jit(solution)/shard_map/exchange_update/pallas_call | solution.py:444
  135.1 34.1 %element_rows.6.part = f32[3072,128]{1,0:T(8,128)} custom-call(f32[2560,128]{1,0:T(8,128)} %get-tuple-element.21.mainface.cur_in.prev_in, f32[512,128]{1,0:T(8,128)} %get-tuple-element.22.ghost.cur_ghost_in.prev_ghost_in, s32[40,512]{1,0:T(8,128)} %get-tuple-element.17.slots_hbm, bf16[256,384]{1,0:T(8,128)(2,1)} %pad_maximum_fusion.mcat, ...), custom_call_target="tpu_custom_call" | custom-call | tf_op jit(solution)/shard_map/element_rows/pallas_call | solution.py:297
  169.2 12.2 %exchange_update.6 = (f32[2560,128]{1,0:T(8,128)}, f32[512,128]{1,0:T(8,128)}) custom-call(f32[3]{0:T(128)} %get-tuple-element.36.coef, f32[3072,128]{1,0:T(8,128)} %element_rows.6.part, f32[2560,128]{1,0:T(8,128)} %get-tuple-element.21.mainface.cur_in.prev_in, f32[512,128]{1,0:T(8,128)} %get-tuple-element.22.ghost.cur_ghost_in.prev_ghost_in, ...), custom_call_target="tpu_custom_call" | custom-call | tf_op jit(solution)/shard_map/exchange_update/pallas_call | solution.py:444
  181.3 33.8 %element_rows.7.part = f32[3072,128]{1,0:T(8,128)} custom-call(f32[2560,128]{1,0:T(8,128)} %get-tuple-element.23.mainface.cur_in, f32[512,128]{1,0:T(8,128)} %get-tuple-element.24.ghost.cur_ghost_in, s32[40,512]{1,0:T(8,128)} %get-tuple-element.17.slots_hbm, bf16[256,384]{1,0:T(8,128)(2,1)} %pad_maximum_fusion.mcat, f32[16,128]{1,0:T(8,128)} %reshape.49.kin, ...), custom_call_target="tpu_custom_call" | custom-call | tf_op jit(solution)/shard_map/element_rows/pallas_call | solution.py:297
  215.2 12.0 %exchange_update.7 = (f32[2560,128]{1,0:T(8,128)}, f32[512,128]{1,0:T(8,128)}) custom-call(f32[3]{0:T(128)} %get-tuple-element.35.coef, f32[3072,128]{1,0:T(8,128)} %element_rows.7.part, f32[2560,128]{1,0:T(8,128)} %get-tuple-element.23.mainface.cur_in, f32[512,128]{1,0:T(8,128)} %get-tuple-element.24.ghost.cur_ghost_in, ...), custom_call_target="tpu_custom_call" | custom-call | tf_op jit(solution)/shard_map/exchange_update/pallas_call | solution.py:444
  227.2 9.4 %final_block.1 = (f32[8,16384]{1,0:T(8,128)}, bf16[4,16,2048]{2,1,0:T(8,128)(2,1)}) custom-call(s32[1]{0:T(128)} %bitcast.core_ref, f32[2560,128]{1,0:T(8,128)} %get-tuple-element.25.mainface, s32[4096]{0:T(1024)} %face_hbm.3, bf16[256,1024]{1,0:T(8,128)(2,1)} %constant.35.clone.emat), custom_call_target="tpu_custom_call" | custom-call | tf_op jit(solution)/shard_map/final_block/pallas_call | solution.py:605
  236.5 22.4 %margin_rows.1 = f32[8,64]{1,0:T(8,128)} custom-call(bf16[4,16,2048]{2,1,0:T(8,128)(2,1)} %get-tuple-element.27.rounded), custom_call_target="tpu_custom_call" | custom-call | tf_op jit(solution)/shard_map/margin_rows/pallas_call | solution.py:550
  259.0 1.3 copy.19
  (28 shorter events, 3.4 us)
Async XLA Ops:
  0.6 10.1 %copy-start = (s32[125,256]{1,0:T(8,128)S(1)}, s32[125,256]{1,0:T(8,128)}, u32[]{:S(2)}) copy-start(s32[125,256]{1,0:T(8,128)} %param.13) | copy-start | bytes 384004
  0.6 12.2 %collective-permute-start = (f32[8,16384]{1,0:T(8,128)}, f32[8,16384]{1,0:T(8,128)S(1)}, u32[]{:S(2)}, u32[]{:S(2)}) collective-permute-start(f32[8,16384]{1,0:T(8,128)} %param.10), channel_id=1, source_target_pairs={{0,1},{1,0},{2,3},{3,2},{4,5},{5,4},{6,7},{7,6},{8,9},{9,8},{10,11... | collective-permute-start | bytes 1572872 | tf_op jit(solution)/shard_map/ppermute | solution.py:665
  9.8 3.0 %copy-start.2 = (f32[256]{0:T(256)S(1)}, f32[256]{0:T(256)}, u32[]{:S(2)}) copy-start(f32[256]{0:T(256)} %param.15) | copy-start | bytes 3076
  9.8 3.0 %copy-start.3 = (f32[256]{0:T(256)S(1)}, f32[256]{0:T(256)}, u32[]{:S(2)}) copy-start(f32[256]{0:T(256)} %param.16) | copy-start | bytes 3076
  10.7 2.1 copy-start.1
  31.5 7.2 %collective-permute-start.1 = (bf16[512,128]{1,0:T(8,128)(2,1)}, bf16[512,128]{1,0:T(8,128)(2,1)S(1)}, u32[]{:S(2)}, u32[]{:S(2)}) collective-permute-start(bf16[512,128]{1,0:T(8,128)(2,1)} %get-tuple-element.16), channel_id=1, source_target_pairs={{8,0},{16,8},{24,16},{32,24},{40,32},{48,40},{56,48},{64,56},{72,6... | collective-permute-start | bytes 393224 | tf_op jit(solution)/shard_map/ppermute | solution.py:670
  32.8 40.6 %collective-permute-start.2 = (bf16[512,128]{1,0:T(8,128)(2,1)}, bf16[512,128]{1,0:T(8,128)(2,1)S(1)}, u32[]{:S(2)}, u32[]{:S(2)}) collective-permute-start(bf16[512,128]{1,0:T(8,128)(2,1)} %get-tuple-element.18), channel_id=1, source_target_pairs={{8,0},{16,8},{24,16},{32,24},{40,32},{48,40},{56,48},{64,56},{72,6... | collective-permute-start | bytes 393224 | tf_op jit(solution)/shard_map/ppermute | solution.py:671

commit v3 on v2

--- a/solution.py
+++ b/solution.py
@@ -103,21 +103,122 @@
     return [lists[j // inside][spots[j % inside]] for j in range(G)]
 
 
-def setup_kernel(
-    nmain, nface, first, second, face_row, face_hbm, raw, emat, out, face_high, face_low, slots, X, sems, *faces
+def states_kernel(
+    nmain, nface, core_ref, own, theirs, face_hbm, emat, out, face_high, face_low, X, sems, *faces
 ):
     qmain, qface = nmain // G, nface // G
     copies = start_faces(face_hbm, faces, sems)
+    core = core_ref[0]
+
+    def turn(i, carry):
+        q = pl.multiple_of(i * 128, 128)
+        parts = []
+        for j in range(G):
+            a = own[:, pl.ds(j * qmain + q, 128)]
+            b = theirs[:, pl.ds(j * qmain + q, 128)]
+            parts += [jnp.where(core == 0, a, b), jnp.where(core == 0, b, a)]
+        out[pl.ds(q, 128), :] = jnp.concatenate(parts, axis=0).T
+        return carry
+
+    lax.fori_loop(0, qmain // 128, turn, 0, unroll=2)
+    expand_section(out, 0, X, 0, qmain, emat)
+    for copy in copies:
+        copy.wait()
+    zero = jnp.zeros((1, LANES), F32)
+
+    def take(q, carry):
+        nodes = faces_at(faces, qface, q)
+        out[pl.ds(qmain + q, 1), :] = merge_groups([X[pl.ds(n, 1), :] for n in nodes])
+        for n in nodes:
+            X[pl.ds(n, 1), :] = zero
+        return carry
+
+    lax.fori_loop(0, qface, take, 0, unroll=8)
+
+    def pack(i, carry):
+        q = pl.multiple_of(i * 8, 8)
+        out[pl.ds(q, 8), :] = merge_groups([X[pl.ds(j * qmain + q, 8), :] for j in range(G)])
+        return carry
+
+    lax.fori_loop(0, qmain // 8, pack, 0, unroll=4)
+    face_high[...], face_low[...] = split(out[qmain : qmain + qface, :])
+
+
+def states_rows(core, own, theirs, face_nodes, emat):
+    nmain, nface = own.shape[1], face_nodes.shape[0]
+    qmain, qface = nmain // G, nface // G
+    vmem = pl.BlockSpec(memory_space=pltpu.VMEM)
+    smem = pl.BlockSpec(memory_space=pltpu.SMEM)
+    return pl.pallas_call(
+        functools.partial(states_kernel, nmain, nface),
+        name="states_rows",
+        out_shape=[
+            jax.ShapeDtypeStruct((qmain + qface, LANES), F32),
+            jax.ShapeDtypeStruct((qface, LANES), BF16),
+            jax.ShapeDtypeStruct((qface, LANES), BF16),
+        ],
+        in_specs=[smem, vmem, vmem, pl.BlockSpec(memory_space=pl.ANY), vmem],
+        out_specs=[vmem, vmem, vmem],
+        scratch_shapes=[
+            pltpu.VMEM((nmain, LANES), F32),
+            pltpu.SemaphoreType.DMA((nface // FACE_LIST,)),
+        ]
+        + [pltpu.SMEM((FACE_LIST,), jnp.int32)] * (nface // FACE_LIST),
+        compiler_params=pltpu.CompilerParams(vmem_limit_bytes=VMEM_LIMIT),
+    )(core, own, theirs, face_nodes, emat)
+
+
+def prepare_kernel(
+    nmain, nface, chunks, after, core_ref, count_ref, bounds, raw, face_rows, matrix, kinetic, potential,
+    slots, scales, mcat, homes, *rest
+):
+    del after
+    coefs, padded = rest[:DEG], rest[DEG]
+    shape = (8, LANES)
+    lowest, lower, upper = (jnp.full(shape, bounds[i], F32) for i in range(3))
+    half_width = (upper - lower) / 2.0
+    center = (upper + lower) / 2.0
+    sigma = half_width / (lowest - center)
+    gamma = 2.0 / sigma
+    coefs[0][...] = jnp.concatenate([sigma / half_width, jnp.zeros(shape, F32), center], axis=0)
+    for k in range(1, DEG):
+        following = 1.0 / (gamma - sigma)
+        coefs[k][...] = jnp.concatenate(
+            [2.0 * following / half_width, sigma * following, center], axis=0
+        )
+        sigma = following
+    core, count = core_ref[0], count_ref[0]
+    place = lax.broadcasted_iota(jnp.int32, (1, LANES), 1)
+    alive = (core * LANES + place) < count
+    lane = lax.broadcasted_iota(jnp.int32, (chunks, LANES), 1)
+    chunk = lax.broadcasted_iota(jnp.int32, (chunks, LANES), 0)
+    spread = (
+        lax.broadcasted_iota(jnp.int32, (LANES, LANES), 0) // chunks
+        == lax.broadcasted_iota(jnp.int32, (LANES, LANES), 1) // W
+    ).astype(F32)
+    for i, (scale, factor) in enumerate(((kinetic, 0.5), (potential, 1.0))):
+        row = jnp.where(core == 0, scale[0:1, :], scale[1:2, :]) * factor
+        row = jnp.where(alive, row, 0.0)
+        wide = jnp.where(lax.rem(lane, chunks) == chunk, row, 0.0)
+        scales[i * chunks : (i + 1) * chunks, :] = jnp.dot(
+            wide, spread, precision=lax.Precision.HIGHEST, preferred_element_type=F32
+        )
+    npe = matrix.shape[1]
+    padded[...] = jnp.zeros_like(padded)
+    padded[0:npe, 0:npe] = matrix[0:npe, :]
+    padded[128 : 128 + npe, 0:npe] = matrix[npe : 2 * npe, :]
+    high, low = split(padded[...])
+    mcat[...] = jnp.concatenate([high, low, high], axis=1)
     hi_count = nmain // 128
-    chunk = 1024
+    size = 1024
     table = jnp.zeros((256, hi_count), F32)
-    for at in range(0, nface, chunk):
+    for at in range(0, nface, size):
         node = jnp.concatenate(
-            [face_row[r : r + 1, :] for r in range(at // 128, (at + chunk) // 128)], axis=1
-        )
-        pos = lax.broadcasted_iota(jnp.int32, (1, chunk), 1) + (at + 1)
-        low = lax.broadcasted_iota(jnp.int32, (128, chunk), 0) == (node & 127)
-        high = lax.broadcasted_iota(jnp.int32, (hi_count, chunk), 0) == (node >> 7)
+            [face_rows[r : r + 1, :] for r in range(at // 128, (at + size) // 128)], axis=1
+        )
+        pos = lax.broadcasted_iota(jnp.int32, (1, size), 1) + (at + 1)
+        low = lax.broadcasted_iota(jnp.int32, (128, size), 0) == (node & 127)
+        high = lax.broadcasted_iota(jnp.int32, (hi_count, size), 0) == (node >> 7)
         big = jnp.where(low, (pos >> 6).astype(F32), 0.0)
         small = jnp.where(low, (pos & 63).astype(F32), 0.0)
         table += lax.dot_general(
@@ -126,9 +227,16 @@
             (((1,), (1,)), ((), ())),
             preferred_element_type=F32,
         )
+    position = (table[:128] * 64.0 + table[128:]).T.astype(jnp.int32)
+    node = (
+        lax.broadcasted_iota(jnp.int32, (hi_count, 128), 0) * 128
+        + lax.broadcasted_iota(jnp.int32, (hi_count, 128), 1)
+    )
+    homes[...] = jnp.where(position > 0, nmain + position - 1, node)
     table = table.astype(BF16)
     width = raw.shape[1]
     owned = (KU - 1) * G
+    slots[...] = jnp.zeros_like(slots)
     for k in range(owned):
         node = raw[k : k + 1, :]
         high = lax.broadcasted_iota(jnp.int32, (hi_count, width), 0) == (node >> 7)
@@ -136,67 +244,38 @@
         both = got[:128] * 64.0 + got[128:]
         low = lax.broadcasted_iota(jnp.int32, (128, width), 0) == (node & 127)
         pos = jnp.sum(jnp.where(low, both, 0.0), axis=0, keepdims=True).astype(jnp.int32)
-        slots[k : k + 1, :] = jnp.where(pos > 0, nmain + pos - 1, node)
-    slots[owned:, :] = raw[owned:, :] + nface
-    def turn(i, carry):
-        q = pl.multiple_of(i * 128, 128)
-        parts = []
-        for j in range(G):
-            parts.append(first[:, pl.ds(j * qmain + q, 128)])
-            parts.append(second[:, pl.ds(j * qmain + q, 128)])
-        out[pl.ds(q, 128), :] = jnp.concatenate(parts, axis=0).T
-        return carry
-
-    lax.fori_loop(0, qmain // 128, turn, 0)
-    expand_section(out, 0, X, 0, qmain, emat)
-    for copy in copies:
-        copy.wait()
-    zero = jnp.zeros((1, LANES), F32)
-
-    def take(q, carry):
-        nodes = faces_at(faces, qface, q)
-        out[pl.ds(qmain + q, 1), :] = merge_groups([X[pl.ds(n, 1), :] for n in nodes])
-        for n in nodes:
-            X[pl.ds(n, 1), :] = zero
-        return carry
-
-    lax.fori_loop(0, qface, take, 0, unroll=4)
-
-    def pack(i, carry):
-        q = pl.multiple_of(i * 8, 8)
-        out[pl.ds(q, 8), :] = merge_groups([X[pl.ds(j * qmain + q, 8), :] for j in range(G)])
-        return carry
-
-    lax.fori_loop(0, qmain // 8, pack, 0, unroll=4)
-    face_high[...], face_low[...] = split(out[qmain : qmain + qface, :])
-
-
-def setup(first, second, face_nodes, raw, emat):
-    nmain, nface = first.shape[1], face_nodes.shape[0]
-    qmain, qface = nmain // G, nface // G
+        slots[k : k + 1, :width] = jnp.where(pos > 0, nmain + pos - 1, node)
+    slots[owned:, :width] = raw[owned:, :] + nface
+
+
+def prepare(after, core, count, bounds, raw, face_nodes, matrix, kinetic, potential, nmain, chunks):
+    nface = face_nodes.shape[0]
     vmem = pl.BlockSpec(memory_space=pltpu.VMEM)
+    smem = pl.BlockSpec(memory_space=pltpu.SMEM)
+    width = -(-raw.shape[1] // 128) * 128
     return pl.pallas_call(
-        functools.partial(setup_kernel, nmain, nface),
-        name="setup_rows",
+        functools.partial(prepare_kernel, nmain, nface, chunks),
+        name="prepare_lists",
         out_shape=[
-            jax.ShapeDtypeStruct((qmain + qface, LANES), F32),
-            jax.ShapeDtypeStruct((qface, LANES), BF16),
-            jax.ShapeDtypeStruct((qface, LANES), BF16),
-            jax.ShapeDtypeStruct(raw.shape, jnp.int32),
-        ],
-        in_specs=[vmem, vmem, vmem, pl.BlockSpec(memory_space=pl.ANY), vmem, vmem],
-        out_specs=[vmem, vmem, vmem, vmem],
-        scratch_shapes=[
-            pltpu.VMEM((nmain, LANES), F32),
-            pltpu.SemaphoreType.DMA((G * qface // FACE_LIST,)),
+            jax.ShapeDtypeStruct((raw.shape[0], width), jnp.int32),
+            jax.ShapeDtypeStruct((2 * chunks, LANES), F32),
+            jax.ShapeDtypeStruct((256, 384), BF16),
+            jax.ShapeDtypeStruct((nmain // 128, 128), jnp.int32),
         ]
-        + [pltpu.SMEM((FACE_LIST,), jnp.int32)] * (G * qface // FACE_LIST),
+        + [jax.ShapeDtypeStruct((24, LANES), F32)] * DEG,
+        in_specs=[pl.BlockSpec(memory_space=pl.ANY)] + [smem] * 3 + [vmem] * 5,
+        out_specs=[vmem] * (4 + DEG),
+        scratch_shapes=[pltpu.VMEM((256, 128), F32)],
         compiler_params=pltpu.CompilerParams(vmem_limit_bytes=VMEM_LIMIT),
-    )(first, second, face_nodes.reshape(nface // 128, 128), face_nodes, raw, emat)
+        cost_estimate=pl.CostEstimate(flops=10**9, bytes_accessed=2**24, transcendentals=0),
+    )(
+        after, core, count, bounds, raw, face_nodes.reshape(nface // 128, 128), matrix,
+        kinetic.reshape(2, LANES), potential.reshape(2, LANES),
+    )
 
 
 def element_kernel(
-    sections, chunks, steps, mainface, ghost, slots_hbm, mcat, kin, pot, emat, fmat,
+    sections, chunks, steps, mainface, ghost, slots_hbm, mcat, scales, emat, fmat,
     part, X, acc0, acc1, U, Y, sems, *lists,
 ):
     copies = start_lists(slots_hbm, lists, sems)
@@ -204,9 +283,7 @@
 
     def clear(row, count):
         row = pl.multiple_of(row, count)
-        zero = jnp.zeros((count, LANES), F32)
-        acc0[pl.ds(row, count), :] = zero
-        acc1[pl.ds(row, count), :] = zero
+        acc0[pl.ds(row, count), :] = jnp.zeros((count, LANES), F32)
 
     at = 0
     src, src_at = mainface, 0
@@ -245,8 +322,9 @@
         )
         for half in range(2):
             lanes = slice(half * LANES, (half + 1) * LANES)
-            row = pl.ds(2 * c + half, 1)
-            Y[half] = kin[row, :] * prod[:128, lanes] + pot[row, :] * prod[128:, lanes]
+            kin = scales[pl.ds(2 * c + half, 1), :]
+            pot = scales[pl.ds(chunks + 2 * c + half, 1), :]
+            Y[half] = kin * prod[:128, lanes] + pot * prod[128:, lanes]
 
     def loop(*works):
         def step(r, carry):
@@ -257,7 +335,14 @@
 
         lax.fori_loop(0, steps, step, 0, unroll=KU)
 
-    loop((gather, 0))
+    share = -(-acc1.shape[0] // (8 * steps)) * 8
+
+    def wipe(c, half, r):
+        if half == 0:
+            start = pl.multiple_of(jnp.minimum(r * share, acc1.shape[0] - share), 8)
+            acc1[pl.ds(start, share), :] = jnp.zeros((share, LANES), F32)
+
+    loop((gather, 0), (wipe, 0))
 
     def chunk(c, carry):
         product(c)
@@ -288,24 +373,24 @@
         out_at += count
 
 
-def elements(mainface, ghost, slots, mcat, kin, pot, emat, fmat, qmain, steps):
+def elements(mainface, ghost, slots, mcat, scales, emat, fmat, qmain, steps):
     qface = mainface.shape[0] - qmain
     sections = (qmain, qface, ghost.shape[0])
     total = sum(sections)
-    chunks = kin.shape[0]
+    chunks = scales.shape[0] // 2
     vmem = pl.BlockSpec(memory_space=pltpu.VMEM)
     return pl.pallas_call(
         functools.partial(element_kernel, sections, chunks, steps),
         name="element_rows",
         out_shape=jax.ShapeDtypeStruct((total, LANES), F32),
-        in_specs=[vmem, vmem, pl.BlockSpec(memory_space=pl.ANY)] + [vmem] * 5,
+        in_specs=[vmem, vmem, pl.BlockSpec(memory_space=pl.ANY)] + [vmem] * 4,
         out_specs=vmem,
         scratch_shapes=[pltpu.VMEM((G * total, LANES), F32)] * 3
         + [pltpu.VMEM((2, 128, LANES), F32)] * 2
         + [pltpu.SemaphoreType.DMA((KU * G,))]
         + [pltpu.SMEM((slots.shape[1],), jnp.int32)] * (KU * G),
         compiler_params=pltpu.CompilerParams(vmem_limit_bytes=VMEM_LIMIT),
-    )(mainface, ghost, slots, mcat, kin, pot, emat, fmat)
+    )(mainface, ghost, slots, mcat, scales, emat, fmat)
 
 
 def exchange_kernel(
@@ -358,8 +443,7 @@
             device_id=(space, other), device_id_type=MESH,
         ).wait_recv()
 
-    for load in loads:
-        load.wait()
+    loads[0].wait()
     face_mine, ghost_mine = pl.ds(face_at + mine, half), pl.ds(ghost_at + mine, half)
     face_other, ghost_other = pl.ds(face_at + not_mine, half), pl.ds(ghost_at + not_mine, half)
     here, there = pl.ds(mine, half), pl.ds(not_mine, half)
@@ -379,7 +463,9 @@
         side.start()
         sides.append(side)
 
-    gain, damp, center = coef[0], coef[1], coef[2]
+    for load in loads[1:]:
+        load.wait()
+    gain, damp, center = coef[0:1, :], coef[8:9, :], coef[16:17, :]
 
     def step(h, now, before):
         return (h - center * now) * gain - damp * before
@@ -448,7 +534,7 @@
             jax.ShapeDtypeStruct(cur.shape, F32),
             jax.ShapeDtypeStruct(cur_ghost.shape, F32),
         ],
-        in_specs=[pl.BlockSpec(memory_space=pltpu.SMEM)] + [hbm] * 5,
+        in_specs=[pl.BlockSpec(memory_space=pltpu.VMEM)] + [hbm] * 5,
         out_specs=[hbm, hbm],
         scratch_shapes=[
             pltpu.VMEM(part.shape, F32),
@@ -478,7 +564,11 @@
     )(coef, part, cur, cur_ghost, prev, prev_ghost)
 
 
-def margin_kernel(grid, node_total, rounded, out, blocks, gram, sums, across, along, *sems):
+def finish_kernel(
+    grid, qmain, source, homes_hbm, emat, out, margin,
+    face, X, C, rounded, blocks, gram, sums, across, along, load_sem, home_sems, *rest,
+):
+    sems, homes = rest[:8], rest[8:]
     depth, width, ring = grid
     space, state = lax.axis_index("space"), lax.axis_index("state")
     z, x = space // width, lax.rem(space, width)
@@ -488,139 +578,158 @@
     friends = [(space, lax.rem(state + k, ring)) for k in range(1, ring)]
     x_friends = [(z * width + lax.rem(x + k, width), state) for k in range(1, width)]
     z_friends = [(lax.rem(z + k, depth) * width + x, state) for k in range(1, depth)]
+    load = pltpu.make_async_copy(source, face, load_sem)
+    load.start()
+    lists = start_faces(homes_hbm, homes, home_sems)
     barrier = pltpu.get_barrier_semaphore()
     everyone = friends + x_friends + z_friends
     for device in everyone:
         pl.semaphore_signal(barrier, inc=1, device_id=device, device_id_type=MESH)
+    load.wait()
+    share = rounded.shape[1]
+    for i in range(ring):
+        rounded[i] = face[i * share : (i + 1) * share, :].astype(BF16)
     pl.semaphore_wait(barrier, len(everyone))
 
     copies = []
     for k in range(1, chips):
         to = lax.rem(y + k, chips)
         copy = pltpu.make_async_remote_copy(
-            src_ref=rounded.at[to], dst_ref=blocks.at[k],
+            src_ref=rounded.at[core * chips + to], dst_ref=blocks.at[k],
             send_sem=state_send.at[k], recv_sem=state_recv.at[k],
             device_id=(space, 2 * to + core), device_id_type=MESH,
         )
         copy.start()
         copies.append(copy)
-    blocks[0] = rounded[y]
+    blocks[0] = rounded[core * chips + y]
+    qface = source.shape[0] - qmain
+    expand_section(face, 0, X, 0, qmain, emat)
+    expand_section(face, qmain, X, G * qmain, qface, emat)
+    for copy in lists:
+        copy.wait()
     for copy in copies:
         copy.wait()
-    ordered = jnp.concatenate([blocks[lax.rem(y + chips - i, chips)] for i in range(chips)], axis=0)
-    gram[:, : ordered.shape[0]] = lax.dot_general(
-        ordered, ordered, (((1,), (1,)), ((), ())), preferred_element_type=F32
+
+    def place(first, last):
+        def block(i, carry):
+            start = i * 128
+
+            def row(q, inner):
+                nodes = [homes[j][start + q] for j in range(G)]
+                C[pl.ds(q, 1), :] = merge_groups([X[pl.ds(n, 1), :] for n in nodes])
+                return inner
+
+            lax.fori_loop(0, 128, row, 0, unroll=8)
+            turned = C[...].T
+            for j in range(G):
+                a = turned[j * W : j * W + 8]
+                b = turned[j * W + 8 : j * W + 16]
+                columns = pl.ds(pl.multiple_of(j * qmain + start, 128), 128)
+                out[:, columns] = jnp.where(core == 0, a, b)
+            return carry
+
+        lax.fori_loop(first, last, block, 0)
+
+    wide = jnp.concatenate([blocks[lax.rem(y + chips - i, chips)] for i in range(chips)], axis=1)
+    pairs = lax.dot_general(
+        wide, wide, (((0,), (0,)), ((), ())), preferred_element_type=F32
     )
-    gram[:, ordered.shape[0] :] = jnp.zeros_like(gram[:, ordered.shape[0] :])
-
-    def add_up(sources, friends, slots, send, recv):
+    lanes = chips * LANES
+    group = lax.rem(lax.broadcasted_iota(jnp.int32, (W, lanes), 1), LANES) // W
+    rows = []
+    for i in range(chips):
+        terms = [
+            jnp.where(group == j, pairs[i * LANES + j * W : i * LANES + (j + 1) * W, :], 0.0)
+            for j in range(G)
+        ]
+        rows.append(functools.reduce(lambda a, b: a + b, terms))
+    lane = lax.broadcasted_iota(jnp.int32, (lanes, LANES), 0)
+    column = lax.broadcasted_iota(jnp.int32, (lanes, LANES), 1)
+    gather = (lane // LANES * W + lax.rem(lane, W) == column).astype(F32)
+    gram[...] = jnp.dot(
+        jnp.concatenate(rows, axis=0), gather,
+        precision=lax.Precision.HIGHEST, preferred_element_type=F32,
+    )
+
+    def send(sources, friends, slots, send_sem, recv_sem):
         copies = []
         for k, (src, device) in enumerate(zip(sources, friends), 1):
             copy = pltpu.make_async_remote_copy(
-                src_ref=src, dst_ref=slots.at[k], send_sem=send.at[k], recv_sem=recv.at[k],
+                src_ref=src, dst_ref=slots.at[k], send_sem=send_sem.at[k], recv_sem=recv_sem.at[k],
                 device_id=device, device_id_type=MESH,
             )
             copy.start()
             copies.append(copy)
+        return copies
+
+    def collect(copies, slots):
         for copy in copies:
             copy.wait()
-        return functools.reduce(lambda a, b: a + b, [slots[k] for k in range(1, len(friends) + 1)])
+        return functools.reduce(
+            lambda a, b: a + b, [slots[k] for k in range(1, len(copies) + 1)]
+        )
 
     def rows_of(member):
         return pl.ds(pl.multiple_of(member * 8, 8), 8)
 
-    rows = [gram.at[rows_of(device[1]), :] for device in friends]
-    total = gram[rows_of(state), :] + add_up(rows, friends, sums, row_send, row_recv)
+    blocks_left = qmain // 128
+    cut1, cut2 = blocks_left // 3, 2 * blocks_left // 3
+    copies = send(
+        [gram.at[rows_of(device[1]), :] for device in friends], friends, sums, row_send, row_recv
+    )
+    place(0, cut1)
+    total = gram[rows_of(state), :] + collect(copies, sums)
     across[0] = total
-    total = total + add_up([across.at[0]] * (width - 1), x_friends, across, x_send, x_recv)
+    copies = send([across.at[0]] * (width - 1), x_friends, across, x_send, x_recv)
+    place(cut1, cut2)
+    total = total + collect(copies, across)
     along[0] = total
-    total = total + add_up([along.at[0]] * (depth - 1), z_friends, along, z_send, z_recv)
-    out[...] = total[:, : out.shape[1]] * (1.0 / node_total)
-
-
-def margin_of(rounded, node_total):
+    copies = send([along.at[0]] * (depth - 1), z_friends, along, z_send, z_recv)
+    place(cut2, blocks_left)
+    total = total + collect(copies, along)
+    margin[...] = total[:, : margin.shape[1]]
+
+
+def finish(source, homes, emat, qmain):
     ring = lax.axis_size("state")
     parts = lax.axis_size("space")
     width = 4
     depth = parts // width
     chips = ring // 2
     count = 8 * ring
+    total = source.shape[0]
+    share = total // ring
     vmem = pl.BlockSpec(memory_space=pltpu.VMEM)
+    anywhere = pl.BlockSpec(memory_space=pl.ANY)
     sems = [pltpu.SemaphoreType.DMA((n,)) for n in (chips, chips, ring, ring, width, width, depth, depth)]
     return pl.pallas_call(
-        functools.partial(margin_kernel, (depth, width, ring), node_total),
-        name="margin_rows",
-        out_shape=jax.ShapeDtypeStruct((8, count), F32),
-        in_specs=[vmem],
-        out_specs=vmem,
+        functools.partial(finish_kernel, (depth, width, ring), qmain),
+        name="finish_block",
+        out_shape=[
+            jax.ShapeDtypeStruct((8, G * qmain), F32),
+            jax.ShapeDtypeStruct((8, count), F32),
+        ],
+        in_specs=[anywhere, anywhere, vmem],
+        out_specs=[vmem, vmem],
         scratch_shapes=[
-            pltpu.VMEM(rounded.shape, BF16),
+            pltpu.VMEM(source.shape, F32),
+            pltpu.VMEM((G * total, LANES), F32),
+            pltpu.VMEM((128, LANES), F32),
+            pltpu.VMEM((ring, share, LANES), BF16),
+            pltpu.VMEM((chips, share, LANES), BF16),
             pltpu.VMEM((count, LANES), F32),
             pltpu.VMEM((ring, 8, LANES), F32),
             pltpu.VMEM((width, 8, LANES), F32),
             pltpu.VMEM((depth, 8, LANES), F32),
+            pltpu.SemaphoreType.DMA,
+            pltpu.SemaphoreType.DMA((G,)),
         ]
-        + sems,
+        + sems
+        + [pltpu.SMEM((qmain,), jnp.int32)] * G,
         compiler_params=pltpu.CompilerParams(
             collective_id=1, has_side_effects=True, vmem_limit_bytes=VMEM_LIMIT
         ),
-    )(rounded)
-
-
-def final_kernel(qmain, qface, core_ref, mainface, face_hbm, emat, out, rounded, X, R, sems, *faces):
-    copies = start_faces(face_hbm, faces, sems)
-    expand_section(mainface, 0, X, 0, qmain, emat)
-    expand_section(mainface, qmain, R, 0, qface, emat)
-    for copy in copies:
-        copy.wait()
-
-    def put(q, carry):
-        for j, n in enumerate(faces_at(faces, qface, q)):
-            X[pl.ds(n, 1), :] = R[pl.ds(j * qface + q, 1), :]
-        return carry
-
-    lax.fori_loop(0, qface, put, 0, unroll=4)
-    core = core_ref[0]
-
-    def turn(i, carry):
-        q = pl.multiple_of(i * 128, 128)
-        rows = merge_groups([X[pl.ds(j * qmain + q, 128), :] for j in range(G)]).T
-        for j in range(G):
-            a = rows[j * W : j * W + 8]
-            b = rows[j * W + 8 : j * W + 16]
-            out[:, pl.ds(j * qmain + q, 128)] = jnp.where(core == 0, a, b)
-        far = G // 2
-        for j in range(far):
-            a = rows[j * W : (j + 1) * W]
-            b = rows[(far + j) * W : (far + j + 1) * W]
-            rounded[j, :, pl.ds(q, 128)] = jnp.where(core == 0, a, b).astype(BF16)
-        return carry
-
-    lax.fori_loop(0, qmain // 128, turn, 0)
-
-
-def final(core, mainface, face_nodes, emat, qmain):
-    qface = mainface.shape[0] - qmain
-    vmem = pl.BlockSpec(memory_space=pltpu.VMEM)
-    return pl.pallas_call(
-        functools.partial(final_kernel, qmain, qface),
-        name="final_block",
-        out_shape=[
-            jax.ShapeDtypeStruct((8, G * qmain), F32),
-            jax.ShapeDtypeStruct((G // 2, W, qmain), BF16),
-        ],
-        in_specs=[
-            pl.BlockSpec(memory_space=pltpu.SMEM), vmem, pl.BlockSpec(memory_space=pl.ANY), vmem
-        ],
-        out_specs=[vmem, vmem],
-        scratch_shapes=[
-            pltpu.VMEM((G * qmain, LANES), F32),
-            pltpu.VMEM((G * qface, LANES), F32),
-            pltpu.SemaphoreType.DMA((G * qface // FACE_LIST,)),
-        ]
-        + [pltpu.SMEM((FACE_LIST,), jnp.int32)] * (G * qface // FACE_LIST),
-        compiler_params=pltpu.CompilerParams(vmem_limit_bytes=VMEM_LIMIT),
-    )(core, mainface, face_nodes, emat)
+    )(source, homes, emat)
 
 
 def body(states, bounds, element_matrix, elem_nodes, face_nodes, kinetic, potential, elem_count):
@@ -633,51 +742,29 @@
     steps = npe // KU
     qmain = states.shape[1] // G
 
-    alive = (jnp.arange(slot_count, dtype=jnp.int32) < elem_count[0]).astype(F32)
-
-    def lanes_of(scale):
-        mine = lax.dynamic_slice(scale, (core * half,), (half,))
-        return jnp.repeat(mine.reshape(G, chunks).T, W, axis=1)
-
-    kin = lanes_of(0.5 * kinetic * alive)
-    pot = lanes_of(potential * alive)
     mine = lax.dynamic_slice(elem_nodes, (0, core * half), (npe, half))
     raw = mine.reshape(KU, steps, G, chunks).transpose(0, 2, 3, 1).reshape(KU * G, chunks * steps)
-    raw = jnp.pad(raw, ((0, 0), (0, (-raw.shape[1]) % 128)))
-    matrix = jnp.pad(element_matrix.reshape(2, npe, npe), ((0, 0), (0, 128 - npe), (0, 128 - npe)))
-    matrix = matrix.reshape(256, 128)
-    high = lax.reduce_precision(matrix, 8, 7)
-    low = matrix - high
-    mcat = jnp.concatenate([high, low, high], axis=1).astype(BF16)
     emat, fmat = expand_matrix(), fold_matrix()
-
-    lowest, lower, upper = bounds[0], bounds[1], bounds[2]
-    half_width = (upper - lower) / 2.0
-    center = (upper + lower) / 2.0
-    sigma = half_width / (lowest - center)
-    gamma = 2.0 / sigma
-    coefs = [jnp.stack([sigma / half_width, jnp.zeros_like(sigma), center])]
-    for _ in range(DEG - 1):
-        following = 1.0 / (gamma - sigma)
-        coefs.append(jnp.stack([2.0 * following / half_width, sigma * following, center]))
-        sigma = following
+    which = core.reshape(1)
 
     partner = lax.ppermute(states, "state", [(i, i ^ 1) for i in range(members)])
-    first = jnp.where(core == 0, states, partner)
-    second = jnp.where(core == 0, partner, states)
-    cur, face_high, face_low, slots = setup(first, second, face_nodes, raw, emat)
+    cur, face_high, face_low = states_rows(which, states, partner, face_nodes, emat)
     downwards = [(i, i - 1) for i in range(1, parts)]
     ghost_high = lax.ppermute(face_high, "space", downwards).astype(F32)
     ghost_low = lax.ppermute(face_low, "space", downwards).astype(F32)
+    slots, scales, mcat, homes, *coefs = prepare(
+        face_low, which, elem_count, bounds, raw, face_nodes, element_matrix, kinetic, potential,
+        states.shape[1], chunks,
+    )
     prev, prev_ghost = cur, ghost_high + ghost_low
     for k in range(DEG):
         ghost = new_ghost if k else ghost_high
-        part = elements(cur, ghost, slots, mcat, kin, pot, emat, fmat, qmain, steps)
+        part = elements(cur, ghost, slots, mcat, scales, emat, fmat, qmain, steps)
         cur_ghost = ghost if k else prev_ghost
         new, new_ghost = exchange(coefs[k], part, cur, cur_ghost, prev, prev_ghost, qmain)
         prev, prev_ghost, cur = cur, cur_ghost, new
-    filtered, rounded = final(core.reshape(1), cur, face_nodes, emat, qmain)
-    margin = margin_of(rounded, states.shape[1] * parts)
+    filtered, margin = finish(cur, homes.reshape(-1), emat, qmain)
+    margin = margin / (states.shape[1] * parts)
     return filtered, margin
 
 

time: 261 us -> 252 us (0.966)
  between operations: 5.2 us -> 1.43 us
  local copies, waits for them, and re-layouts: 6.99 us -> 3.99 us
  transfers between devices with their start and end apart: 3 -> 3, of which waited for: 1 -> 1; matrix products, arithmetic and copies ran while one was open for 3% -> 1% of each run, Pallas kernels for 13% -> 16%
where the time goes in v3:
time: 252 us; the launch traced here: 251 us
  Pallas kernels  235 us (93%)
  starting transfers between devices  5.91 us (2%)
  local copies, waits for them, and re-layouts  3.99 us (2%)
  other arithmetic  2.73 us (1%)
    pallas_call x4, Pallas kernels, elements(): pl.pallas_call(functools.partial(element_kernel, sections, chunks, steps)...  135 us
    pallas_call x4, Pallas kernels, exchange(): pl.pallas_call(functools.partial(exchange_kernel, qmain, qface, parts), n...  52.3 us
    pallas_call x1, Pallas kernels, finish(): pl.pallas_call(functools.partial(finish_kernel, (depth, width, ring), qma...  29.3 us
    pallas_call x1, Pallas kernels, states_rows(): pl.pallas_call(functools.partial(states_kernel, nmain, nface), name='stat...  11.8 us
    pallas_call x1, Pallas kernels, prepare(): pl.pallas_call(functools.partial(prepare_kernel, nmain, nface, chunks), n...  6.9 us
  transfers between devices with their start and end apart: 3, of which 1 were waited for; matrix products, arithmetic and copies ran while one was open for 1% of the time, Pallas kernels for 16%

profile of v3, /device:TPU:1, one launch (start us, length us, event | category | flops | bytes accessed | tf_op | source)
XLA Modules:
  0.0 251.0 jit_solution(12519980081235004786)
XLA Ops:
  0.6 0.0 copy-start
  0.6 3.3 %collective-permute-start = (f32[8,16384]{1,0:T(8,128)}, f32[8,16384]{1,0:T(8,128)S(1)}, u32[]{:S(2)}, u32[]{:S(2)}) collective-permute-start(f32[8,16384]{1,0:T(8,128)} %own.1), channel_id=1, source_target_pairs={{0,1},{1,0},{2,3},{3,2},{4,5},{5,4},{6,7},{7,6},{8,9},{9,8},{10,11... | collective-permute-start | bytes 1572872 | tf_op jit(solution)/shard_map/ppermute | solution.py:750
  4.0 1.7 collective-permute-done.theirs
  5.7 0.8 copy-done.1
  6.5 11.8 %states_rows.1 = (f32[2560,128]{1,0:T(8,128)}, bf16[512,128]{1,0:T(8,128)(2,1)}, bf16[512,128]{1,0:T(8,128)(2,1)}) custom-call(s32[1]{0:T(128)} %bitcast.core_ref, f32[8,16384]{1,0:T(8,128)} %own.1, f32[8,16384]{1,0:T(8,128)} %copy-done.1, s32[4096]{0:T(1024)} %face_hbm.1, bf16[256,1024]{1,0:T(8,128)(2,1)} %constant.21.clone.emat), custom_call_target="tpu_custom_call" | custom-call | tf_op jit(solution)/shard_map/states_rows/pallas_call | solution.py:152
  18.4 1.3 collective-permute-start.1
  19.7 1.3 collective-permute-start.2
  21.6 0.2 reshape.26
  21.8 0.3 copy.12
  22.1 0.8 reshape.27.raw
  23.0 6.9 %prepare_lists.1 = (s32[40,512]{1,0:T(8,128)}, f32[32,128]{1,0:T(8,128)}, bf16[256,384]{1,0:T(8,128)(2,1)}, s32[128,128]{1,0:T(8,128)}, f32[24,128]{1,0:T(8,128)...) custom-call(bf16[512,128]{1,0:T(8,128)(2,1)} %get-tuple-element.22.after, s32[1]{0:T(128)} %bitcast.core_ref, ...), custom_call_target="tpu_custom_call" | custom-call | flops 1000000000 | bytes 16777216 | tf_op jit(solution)/shard_map/prepare_lists/pallas_call | solution.py:256
  29.9 0.7 convert_element_type.6.ghost
  30.6 33.8 %element_rows.4.part = f32[3072,128]{1,0:T(8,128)} custom-call(f32[2560,128]{1,0:T(8,128)} %get-tuple-element.27.mainface.cur_in.prev_in, f32[512,128]{1,0:T(8,128)} %convert_element_type.6.ghost, s32[40,512]{1,0:T(8,128)} %get-tuple-element.29.slots_hbm, bf16[256,384]{1,0:T(8,128)(2,1)} %get-tuple-element.30.mcat, f32[32,128]{1,0:T(8,128)} %get-tuple-element.31.scales, ...), custom_call_target="tpu_custom_call" | custom-call | tf_op jit(solution)/shard_map/element_rows/pallas_call | solution.py:382
  64.4 0.7 convert_add_fusion.cur_ghost_in.prev_ghost_in
  65.1 16.4 %exchange_update.4 = (f32[2560,128]{1,0:T(8,128)}, f32[512,128]{1,0:T(8,128)}) custom-call(f32[24,128]{1,0:T(8,128)} %get-tuple-element.26.coef, f32[3072,128]{1,0:T(8,128)} %element_rows.4.part, f32[2560,128]{1,0:T(8,128)} %get-tuple-element.27.mainface.cur_in.prev_in, f32[512,128]{1,0:T(8,128)} %convert_add_fusion.cur_ghost_in.prev_ghost_in, ...), custom_call_target="tpu_custom_call" | custom-call | tf_op jit(solution)/shard_map/exchange_update/pallas_call | solution.py:530
  81.6 33.6 %element_rows.5.part = f32[3072,128]{1,0:T(8,128)} custom-call(f32[2560,128]{1,0:T(8,128)} %get-tuple-element.32.mainface.cur_in.prev_in, f32[512,128]{1,0:T(8,128)} %get-tuple-element.33.ghost.cur_ghost_in.prev_ghost_in, s32[40,512]{1,0:T(8,128)} %get-tuple-element.29.slots_hbm, bf16[256,384]{1,0:T(8,128)(2,1)} %get-tuple-element.30.mcat, ...), custom_call_target="tpu_custom_call" | custom-call | tf_op jit(solution)/shard_map/element_rows/pallas_call | solution.py:382
  115.2 12.2 %exchange_update.5 = (f32[2560,128]{1,0:T(8,128)}, f32[512,128]{1,0:T(8,128)}) custom-call(f32[24,128]{1,0:T(8,128)} %get-tuple-element.25.coef, f32[3072,128]{1,0:T(8,128)} %element_rows.5.part, f32[2560,128]{1,0:T(8,128)} %get-tuple-element.32.mainface.cur_in.prev_in, f32[512,128]{1,0:T(8,128)} %get-tuple-element.33.ghost.cur_ghost_in.prev_ghost_in, ...), custom_call_target="tpu_custom_call" | custom-call | tf_op jit(solution)/shard_map/exchange_update/pallas_call | solution.py:530
  127.3 33.8 %element_rows.6.part = f32[3072,128]{1,0:T(8,128)} custom-call(f32[2560,128]{1,0:T(8,128)} %get-tuple-element.34.mainface.cur_in.prev_in, f32[512,128]{1,0:T(8,128)} %get-tuple-element.35.ghost.cur_ghost_in.prev_ghost_in, s32[40,512]{1,0:T(8,128)} %get-tuple-element.29.slots_hbm, bf16[256,384]{1,0:T(8,128)(2,1)} %get-tuple-element.30.mcat, ...), custom_call_target="tpu_custom_call" | custom-call | tf_op jit(solution)/shard_map/element_rows/pallas_call | solution.py:382
  161.2 11.9 %exchange_update.6 = (f32[2560,128]{1,0:T(8,128)}, f32[512,128]{1,0:T(8,128)}) custom-call(f32[24,128]{1,0:T(8,128)} %get-tuple-element.24.coef, f32[3072,128]{1,0:T(8,128)} %element_rows.6.part, f32[2560,128]{1,0:T(8,128)} %get-tuple-element.34.mainface.cur_in.prev_in, f32[512,128]{1,0:T(8,128)} %get-tuple-element.35.ghost.cur_ghost_in.prev_ghost_in, ...), custom_call_target="tpu_custom_call" | custom-call | tf_op jit(solution)/shard_map/exchange_update/pallas_call | solution.py:530
  173.1 33.6 %element_rows.7.part = f32[3072,128]{1,0:T(8,128)} custom-call(f32[2560,128]{1,0:T(8,128)} %get-tuple-element.36.mainface.cur_in, f32[512,128]{1,0:T(8,128)} %get-tuple-element.37.ghost.cur_ghost_in, s32[40,512]{1,0:T(8,128)} %get-tuple-element.29.slots_hbm, bf16[256,384]{1,0:T(8,128)(2,1)} %get-tuple-element.30.mcat, f32[32,128]{1,0:T(8,128)} %get-tuple-element.31.scales, ...), custom_call_target="tpu_custom_call" | custom-call | tf_op jit(solution)/shard_map/element_rows/pallas_call | solution.py:382
  206.7 11.8 %exchange_update.7 = (f32[2560,128]{1,0:T(8,128)}, f32[512,128]{1,0:T(8,128)}) custom-call(f32[24,128]{1,0:T(8,128)} %get-tuple-element.23.coef, f32[3072,128]{1,0:T(8,128)} %element_rows.7.part, f32[2560,128]{1,0:T(8,128)} %get-tuple-element.36.mainface.cur_in, f32[512,128]{1,0:T(8,128)} %get-tuple-element.37.ghost.cur_ghost_in, ...), custom_call_target="tpu_custom_call" | custom-call | tf_op jit(solution)/shard_map/exchange_update/pallas_call | solution.py:530
  218.6 29.3 %finish_block.1 = (f32[8,16384]{1,0:T(8,128)}, f32[8,64]{1,0:T(8,128)}) custom-call(f32[2560,128]{1,0:T(8,128)} %get-tuple-element.38.source, s32[16384]{0:T(1024)} %bitcast.9, bf16[256,1024]{1,0:T(8,128)(2,1)} %constant.21.clone.emat), custom_call_target="tpu_custom_call" | custom-call | tf_op jit(solution)/shard_map/finish_block/pallas_call | solution.py:705
  247.8 1.3 broadcast_multiply_fusion
  249.1 1.9 copy.15
  (5 shorter events, 0.0 us)
Async XLA Ops:
  0.6 20.3 %copy-start = (s32[125,256]{1,0:T(8,128)S(1)}, s32[125,256]{1,0:T(8,128)}, u32[]{:S(2)}) copy-start(s32[125,256]{1,0:T(8,128)} %param.13) | copy-start | bytes 384004
  0.6 5.1 %collective-permute-start = (f32[8,16384]{1,0:T(8,128)}, f32[8,16384]{1,0:T(8,128)S(1)}, u32[]{:S(2)}, u32[]{:S(2)}) collective-permute-start(f32[8,16384]{1,0:T(8,128)} %own.1), channel_id=1, source_target_pairs={{0,1},{1,0},{2,3},{3,2},{4,5},{5,4},{6,7},{7,6},{8,9},{9,8},{10,11... | collective-permute-start | bytes 1572872 | tf_op jit(solution)/shard_map/ppermute | solution.py:750
  5.7 0.8 copy-start.1
  18.4 11.5 %collective-permute-start.1 = (bf16[512,128]{1,0:T(8,128)(2,1)}, bf16[512,128]{1,0:T(8,128)(2,1)S(1)}, u32[]{:S(2)}, u32[]{:S(2)}) collective-permute-start(bf16[512,128]{1,0:T(8,128)(2,1)} %get-tuple-element.28), channel_id=1, source_target_pairs={{8,0},{16,8},{24,16},{32,24},{40,32},{48,40},{56,48},{64,56},{72,6... | collective-permute-start | bytes 393224 | tf_op jit(solution)/shard_map/ppermute | solution.py:753
  19.7 44.7 %collective-permute-start.2 = (bf16[512,128]{1,0:T(8,128)(2,1)}, bf16[512,128]{1,0:T(8,128)(2,1)S(1)}, u32[]{:S(2)}, u32[]{:S(2)}) collective-permute-start(bf16[512,128]{1,0:T(8,128)(2,1)} %get-tuple-element.22.after), channel_id=1, source_target_pairs={{8,0},{16,8},{24,16},{32,24},{40,32},{48,40},{56,48},{64,56},{72,6... | collective-permute-start | bytes 393224 | tf_op jit(solution)/shard_map/ppermute | solution.py:754
